TPU v7x, 32 devices: a whole 2x2x4 slice. The times are simulated.
32 devices in a mesh: seq: 8 (over z, core), img: 4 (over y, x).
Axes of the slice: x: 2, y: 2, z: 4, core: 2. Of those that a mesh axis runs over, the one named last changes fastest.
Arguments:
- tokens: bfloat16 [4, 24, 128, 2240], P('img', 'seq'), may hold values from -8 to 8
- norm_gain: bfloat16 [2240], replicated, may hold values from 0.099609375 to 1.8984375
- caption: bfloat16 [4, 2240], P('img'), may hold values from -6 to 6
- null_caption: bfloat16 [2240], replicated, may hold values from -6 to 6
- keep: int32 [4], P('img'), may hold values from 0 to 1, as said below
- bucket_rows: int32 [4], P('img'), may hold values from 7 to 24, as said below
- w_qkv: bfloat16 [2240, 3456], P('img', 'seq'), may hold values from -0.125 to 0.125
Outputs:
- attended: bfloat16 [4, 24, 128, 1152], P('img', 'seq')
Inputs may be any that keep to these rules, and one draw needn't show every extreme that they name: `keep`: 1 keeps the image's caption, 0 drops it; some image keeps and some drops. `bucket_rows`: rows in use are the first ones of an image's grid; some image uses all 24 rows.
All inputs are finite; a program needn't handle non-finite values.
Results may differ from a plain program's by a relative error of at most 0.0017.
Values may be sent and summed in bfloat16 or wider, within the bound.
A program may use at most 128 MiB of HBM per device.

v0:
```python
import jax
import jax.numpy as jnp
from jax import lax
from jax.sharding import PartitionSpec as P

HDIM = 32


norm_eps = 1e-06
attn_eps = 1e-06


def body(tokens, norm_gain, caption, null_caption, keep, bucket_rows, w_qkv):
    grid_rows = tokens.shape[1]
    grid_cols = tokens.shape[2]
    features_count = tokens.shape[3]
    token_count = grid_rows * grid_cols
    features = tokens.reshape(token_count, features_count).astype(jnp.float32)
    mean_square = jnp.mean(features * features, axis=1, keepdims=True)
    condition = jnp.where(keep[0] > 0, caption[0], null_caption).astype(jnp.float32)
    hidden = (
        features * lax.rsqrt(mean_square + norm_eps) * norm_gain.astype(jnp.float32) + condition
    ).astype(jnp.bfloat16)
    rows_whole = lax.all_gather(w_qkv, "img", axis=0, tiled=True)
    projected = jnp.dot(
        hidden,
        lax.all_gather(rows_whole, "seq", axis=1, tiled=True),
        preferred_element_type=jnp.float32,
    )
    inner_width = projected.shape[1] // 3
    head_count = inner_width // HDIM
    grid_row = (
        lax.axis_index("seq") * grid_rows + jnp.arange(token_count, dtype=jnp.int32) // grid_cols
    )
    live_mask = (grid_row < bucket_rows[0]).astype(jnp.float32)
    queries = jax.nn.relu(projected[:, :inner_width]).reshape(token_count, head_count, HDIM)
    keys_relu = jax.nn.relu(projected[:, inner_width : 2 * inner_width]).reshape(
        token_count, head_count, HDIM
    )
    keys_relu = keys_relu * live_mask[:, None, None]
    values = projected[:, 2 * inner_width :].reshape(token_count, head_count, HDIM)
    state_outer = jnp.einsum("thd,the->hde", keys_relu, values, precision=lax.Precision.HIGHEST)
    key_total = jnp.sum(keys_relu, axis=0)
    state_outer, key_total = lax.psum((state_outer, key_total), "seq")
    numerator = jnp.einsum("thd,hde->the", queries, state_outer, precision=lax.Precision.HIGHEST)
    denominator = jnp.einsum("thd,hd->th", queries, key_total, precision=lax.Precision.HIGHEST)
    result = numerator / (denominator[:, :, None] + attn_eps) * live_mask[:, None, None]
    return result.reshape(1, grid_rows, grid_cols, inner_width).astype(jnp.bfloat16)


def solution(mesh):
    in_specs = (
        P("img", "seq", None, None),
        P(),
        P("img", None),
        P(),
        P("img"),
        P("img"),
        P("img", "seq"),
    )
    out_specs = P("img", "seq", None, None)
    return jax.shard_map(body, mesh=mesh, in_specs=in_specs, out_specs=out_specs, check_vma=False)
```

profile of v0, /device:TPU:0, one launch (start us, length us, event | category | flops | bytes accessed | tf_op | source)
XLA Modules:
  0.0 313.0 jit_solution(10901783055646727435)
XLA Ops:
  6.5 0.0 all-gather.6.cloned.1.call-start
  6.5 0.7 all-gather.6.cloned.1.call-update
  7.3 0.0 all-gather.4.cloned.1.call-start
  7.3 40.9 %all-gather.6.cloned.1.call-done = bf16[4,560,432]{1,2,0:T(8,128)(2,1)} async-done(((bf16[1,560,432]{1,2,0:T(8,128)(2,1)}), bf16[4,560,432]{1,2,0:T(8,128)(2,1)}) %all-gather.6.cloned.1.call-update) | async-done | bytes 1935376 | tf_op jit(solution)/shard_map/all_gather | solution.py:24
  48.2 2.5 copy.18
  50.7 2.7 reshape.71
  53.4 0.0 copy-start.1
  53.4 0.0 all-gather.4.cloned.1.call-update
  53.4 0.0 all-reduce.2.cloned.1.call-start
  54.8 0.0 copy-done.1
  54.8 2.6 copy.17
  57.4 1.3 reduce.2
  58.8 1.9 multiply_reduce_fusion
  60.7 0.7 select_convert_fusion
  61.4 1.7 fusion.2
  63.1 134.6 %all-gather.4.cloned.1.call-done = bf16[2240,3456]{0,1:T(8,128)(2,1)} async-done(((bf16[2240,432]{0,1:T(8,128)(2,1)}), bf16[2240,3456]{0,1:T(8,128)(2,1)}) %all-gather.4.cloned.1.call-update) | async-done | bytes 15482896 | tf_op jit(solution)/shard_map/all_gather | solution.py:27
  197.7 10.8 %fusion.17 = f32[384,3456]{1,0:T(8,128)S(1)} fusion(bf16[384,2240]{1,0:T(8,128)(2,1)} %fusion.2, bf16[2240,3456]{0,1:T(8,128)(2,1)} %all-gather.4.cloned.1.call-done), kind=kOutput, calls=%fused_computation.30 | convolution fusion | flops 5945425920 | bytes 22511616 | tf_op jit(solution)/shard_map/dot_general | solution.py:25
  208.6 1.6 multiply_reduce_fusion.1
  210.2 0.7 reduce_sum.22
  210.9 27.3 %psum.15 = f32[36,32]{1,0:T(8,128)} all-reduce(f32[36,32]{1,0:T(8,128)} %reduce_sum.22), channel_id=1, replica_groups=mesh['seq'=8,'img'=4] {'seq'}, use_global_device_ids=true, to_apply=%region_3.4 | all-reduce | flops 1152 | bytes 9216 | tf_op jit(solution)/shard_map/psum | solution.py:44
  238.2 1.8 copy.21
  239.9 1.2 copy.20
  241.1 2.2 copy.19
  243.3 3.0 fusion.5
  246.3 0.0 copy-start
  246.3 0.0 all-reduce.2.cloned.1.call-update
  246.3 2.7 fusion.9
  249.1 52.3 %all-reduce.2.cloned.1.call-done = f32[36,32,32]{2,1,0:T(8,128)} async-done(((f32[36,32,32]{2,1,0:T(8,128)}), f32[36,32,32]{2,1,0:T(8,128)}) %all-reduce.2.cloned.1.call-update) | async-done | bytes 147472 | tf_op jit(solution)/shard_map/psum | solution.py:44
  301.4 0.0 copy-done
  301.4 2.8 fusion.4
  304.2 0.3 convert_element_type.47
  304.5 1.9 copy.23
  (4 shorter events, 0.0 us)
Async XLA Ops:
  6.5 41.7 %all-gather.6.cloned.1.call-start = ((), (), s32[]{:S(2)}) async-start(), calls=%async_computation.2 | async-start | bytes 2764800 | tf_op jit(solution)/shard_map/all_gather | solution.py:24
  7.3 190.5 %all-gather.4.cloned.1.call-start = ((), (), s32[]{:S(2)}) async-start(), calls=%async_computation | async-start | bytes 17915904 | tf_op jit(solution)/shard_map/all_gather | solution.py:27
  53.4 1.4 copy-start.1
  53.4 247.9 %all-reduce.2.cloned.1.call-start = ((), (), s32[]{:S(2)}) async-start(), calls=%async_computation.1 | async-start | bytes 1179648 | tf_op jit(solution)/shard_map/psum | solution.py:44
  246.3 55.1 %copy-start = (f32[384,1152]{0,1:T(8,128)S(1)}, f32[384,1152]{0,1:T(8,128)}, u32[]{:S(2)}) copy-start(f32[384,1152]{0,1:T(8,128)} %copy.21) | copy-start | bytes 5308420
Sparse Core Ops, SparseCore 0:
  9.2 38.9 all-gather.5
  53.5 144.1 all-gather.3
  246.4 54.8 all-reduce.1
where the time goes:
time: 313 us
  waiting for transfers between devices  228 us (73%)
  blocking collectives  27.3 us (9%)
  matrix products  19.4 us (6%)
  local copies, waits for them, and re-layouts  15.9 us (5%)
  between operations  14.5 us (5%)
  other arithmetic  7.35 us (2%)
    all_gather x1, waiting for transfers between devices, body(): lax.all_gather(rows_whole, 'seq', axis=1, tiled=True)  135 us
    psum x1, waiting for transfers between devices, body(): state_outer, key_total = lax.psum((state_outer, key_total), 'seq')  52.3 us
    all_gather x1, waiting for transfers between devices, body(): rows_whole = lax.all_gather(w_qkv, 'img', axis=0, tiled=True)  40.9 us
    psum x1, blocking collectives, body(): state_outer, key_total = lax.psum((state_outer, key_total), 'seq')  27.3 us
    dot_general x1, matrix products, body(): jnp.dot(hidden, lax.all_gather(rows_whole, 'seq', axis=1, tiled=True), pr...  10.8 us
  transfers between devices with their start and end apart: 3, of which 3 were waited for; matrix products, arithmetic and copies ran while one was open for 4% of the time, Pallas kernels for 0%

commit v1 on v0

--- a/solution.py
+++ b/solution.py
@@ -1,13 +1,322 @@
+import functools
+
 import jax
 import jax.numpy as jnp
 from jax import lax
+from jax.experimental import pallas as pl
+from jax.experimental.pallas import tpu as pltpu
 from jax.sharding import PartitionSpec as P
 
 HDIM = 32
-
+LANES = 128
+PARTS = 2
 
 norm_eps = 1e-06
 attn_eps = 1e-06
+HIGHEST = lax.Precision.HIGHEST
+
+
+def gray(r):
+    return r + r // 2 - 2 * (r // 3)
+
+
+def kernel(
+    dims,
+    tokens_ref, gain_ref, caption_ref, null_ref, keep_ref, rows_ref, w_ref,
+    out_ref,
+    own, wbuf, hid, proj, full, state, pieces, total,
+    send_sems, z_sems, left_sems, right_sems, far_sems, twin_sems, piece_sems, total_sems, local_sem,
+):
+    n_img, n_seq, grid_rows, grid_cols, depth, width, inner = dims
+    main_tiles = width // LANES
+    main = main_tiles * LANES
+    tail = width - main
+    deep_tiles = -(-depth // LANES)
+    packed = own.shape[0]
+    part_rows = packed // PARTS
+    n_z = n_seq // 2
+    token_count = grid_rows * grid_cols
+
+    seq = lax.axis_index("seq")
+    img = lax.axis_index("img")
+    core = lax.rem(seq, 2)
+    z = seq // 2
+    ring = gray(img)
+    right = gray(lax.rem(ring + 1, 4))
+    left = gray(lax.rem(ring + 3, 4))
+    far = gray(lax.rem(ring + 2, 4))
+    twin = seq + 1 - 2 * core
+    zs = [z, z + 1 - 2 * lax.rem(z, 2), lax.rem(z + 2, 4), 3 - z]
+    mine = [2 * q + core for q in zs]
+    twins = [2 * q + 1 - core for q in zs]
+
+    barrier = pltpu.get_barrier_semaphore()
+    peers = [(img, lax.rem(seq + d, n_seq)) for d in range(1, n_seq)] + [(left, seq), (right, seq)]
+    for i, s in peers:
+        pl.semaphore_signal(
+            barrier, inc=1, device_id={"img": i, "seq": s}, device_id_type=pl.DeviceIdType.MESH
+        )
+
+    for j in range(main_tiles):
+        own[depth * j : depth * (j + 1), :] = w_ref[:, LANES * j : LANES * (j + 1)]
+    rows_at = lax.broadcasted_iota(jnp.int32, (tail, tail), 0)
+    cols_at = lax.broadcasted_iota(jnp.int32, (tail, tail), 1)
+    unit = (rows_at == cols_at).astype(jnp.bfloat16)
+    rest = lax.dot_general(
+        unit, w_ref[:, main:width], (((1,), (1,)), ((), ())), preferred_element_type=jnp.float32
+    ).astype(jnp.bfloat16)
+    base = depth * main_tiles
+    for j in range(deep_tiles):
+        lanes = min(LANES, depth - LANES * j)
+        if lanes < LANES:
+            own[base + tail * j : base + tail * (j + 1), :] = jnp.zeros((tail, LANES), jnp.bfloat16)
+        own[base + tail * j : base + tail * (j + 1), 0:lanes] = rest[:, LANES * j : LANES * j + lanes]
+
+    pl.semaphore_wait(barrier, len(peers))
+
+    sends = []
+
+    def part(p):
+        return pl.ds(p * part_rows, part_rows)
+
+    def send(src, i, s, p, recv_sem, to_img, to_seq):
+        copy = pltpu.make_async_remote_copy(
+            src_ref=src,
+            dst_ref=wbuf.at[i, s, part(p)],
+            send_sem=send_sems.at[len(sends)],
+            recv_sem=recv_sem,
+            device_id={"img": to_img, "seq": to_seq},
+            device_id_type=pl.DeviceIdType.MESH,
+        )
+        copy.start()
+        sends.append(copy)
+
+    def arrive(i, s, p, recv_sem):
+        block = wbuf.at[i, s, part(p)]
+        pltpu.make_async_remote_copy(
+            src_ref=block, dst_ref=block, send_sem=send_sems.at[0], recv_sem=recv_sem,
+            device_id={"img": img, "seq": twin}, device_id_type=pl.DeviceIdType.MESH,
+        ).wait_recv()
+        return block
+
+    keep_own = pltpu.make_async_copy(own, wbuf.at[img, seq], local_sem)
+    keep_own.start()
+    for p in range(PARTS):
+        src = own.at[part(p)]
+        send(src, img, seq, p, left_sems.at[0, p], right, seq)
+        send(src, img, seq, p, right_sems.at[0, p], left, seq)
+        send(src, img, seq, p, z_sems.at[0, p], img, mine[1])
+        send(src, img, seq, p, twin_sems.at[0, 0, p], img, twin)
+    for k in range(2, n_z):
+        for p in range(PARTS):
+            send(own.at[part(p)], img, seq, p, z_sems.at[k - 1, p], img, mine[k])
+
+    keep_flag = (keep_ref[0] > 0).astype(jnp.float32)
+    condition = jnp.where(
+        jnp.full((1, depth * n_img), keep_flag) > 0.5,
+        caption_ref[...].astype(jnp.float32),
+        null_ref[...].astype(jnp.float32),
+    )
+    gain = gain_ref[...].astype(jnp.float32)
+    deep = deep_tiles * LANES
+    if deep > depth:
+        hid[:, :, deep - LANES :] = jnp.zeros((n_img, token_count, LANES), jnp.bfloat16)
+    step_rows = 32
+
+    @pl.loop(0, token_count // step_rows)
+    def _(t):
+        rows = pl.ds(pl.multiple_of(t * step_rows, step_rows), step_rows)
+        features = tokens_ref[rows, :].astype(jnp.float32)
+        mean_square = jnp.mean(features * features, axis=1, keepdims=True)
+        hidden = (features * lax.rsqrt(mean_square + norm_eps) * gain + condition).astype(jnp.bfloat16)
+        for i in range(n_img):
+            hid[i, rows, 0:depth] = hidden[:, depth * i : depth * (i + 1)]
+
+    keep_own.wait()
+
+    def project(s):
+        @pl.loop(0, grid_rows)
+        def _(t):
+            rows = pl.ds(pl.multiple_of(t * grid_cols, grid_cols), grid_cols)
+            acc = jnp.zeros((grid_cols, main), jnp.float32)
+            acc_tail = jnp.zeros((grid_cols, tail), jnp.float32)
+            for i in range(n_img):
+                block = jnp.concatenate(
+                    [wbuf[i, s, depth * j : depth * (j + 1), :] for j in range(main_tiles)], axis=1
+                )
+                acc += jnp.dot(hid[i, rows, 0:depth], block, preferred_element_type=jnp.float32)
+                ends = jnp.concatenate(
+                    [wbuf[i, s, base + tail * j : base + tail * (j + 1), :] for j in range(deep_tiles)],
+                    axis=1,
+                )
+                acc_tail += lax.dot_general(
+                    hid[i, rows, :], ends, (((1,), (1,)), ((), ())), preferred_element_type=jnp.float32
+                )
+            proj[s, rows, 0:main] = acc
+            proj[s, rows, main:width] = acc_tail
+
+    def finish(k):
+        for p in range(PARTS):
+            for at, i in enumerate((img, left, right)):
+                arrive(i, twins[k], p, twin_sems.at[k, at, p])
+        arrive(far, twins[k], 0, twin_sems.at[k, 3, 0])
+        arrive(far, twins[k], 1, twin_sems.at[k, 3, 1])
+        project(mine[k])
+        project(twins[k])
+
+    for k in range(n_z):
+        if k + 1 < n_z:
+            s = mine[k + 1]
+            for p in range(PARTS):
+                src = arrive(img, s, p, z_sems.at[k, p])
+                send(src, img, s, p, left_sems.at[k + 1, p], right, seq)
+                send(src, img, s, p, right_sems.at[k + 1, p], left, seq)
+                send(src, img, s, p, twin_sems.at[k + 1, 0, p], img, twin)
+        s = mine[k]
+        for p in range(PARTS):
+            src = arrive(left, s, p, left_sems.at[k, p])
+            if p == 0:
+                send(src, left, s, p, far_sems.at[k, 0], right, seq)
+            send(src, left, s, p, twin_sems.at[k, 1, p], img, twin)
+            src = arrive(right, s, p, right_sems.at[k, p])
+            if p == 1:
+                send(src, right, s, p, far_sems.at[k, 1], left, seq)
+            send(src, right, s, p, twin_sems.at[k, 2, p], img, twin)
+        if k > 0:
+            finish(k - 1)
+        for p in range(PARTS):
+            src = arrive(far, s, p, far_sems.at[k, p])
+            send(src, far, s, p, twin_sems.at[k, 3, p], img, twin)
+    finish(n_z - 1)
+
+    @pl.loop(0, grid_rows)
+    def _(t):
+        rows = pl.ds(pl.multiple_of(t * grid_cols, grid_cols), grid_cols)
+        for s in range(n_seq):
+            full[rows, width * s : width * (s + 1)] = proj[s, rows, 0:width]
+
+    groups = inner // LANES
+    head_of_row = lax.broadcasted_iota(jnp.int32, (LANES, LANES), 0) // HDIM
+    head_of_col = lax.broadcasted_iota(jnp.int32, (LANES, LANES), 1) // HDIM
+    same = (head_of_row == head_of_col).astype(jnp.float32)
+    live_rows = seq * grid_rows + lax.broadcasted_iota(jnp.int32, (token_count, LANES), 0) // grid_cols
+    live = (live_rows < rows_ref[0]).astype(jnp.float32)
+    state[...] = jnp.zeros_like(state)
+    for g in range(groups):
+        keys = jax.nn.relu(full[:, inner + LANES * g : inner + LANES * (g + 1)]) * live
+        values = full[:, 2 * inner + LANES * g : 2 * inner + LANES * (g + 1)]
+        outer = lax.dot_general(
+            keys, values, (((0,), (0,)), ((), ())), precision=HIGHEST, preferred_element_type=jnp.float32
+        ) * same
+        state[HDIM * g : HDIM * (g + 1), :] = (
+            outer[0:32] + outer[32:64] + outer[64:96] + outer[96:128]
+        )
+        state[HDIM * groups + g : HDIM * groups + g + 1, :] = jnp.sum(keys, axis=0, keepdims=True)
+
+    piece = state.shape[0] // n_seq
+
+    def piece_of(ref, s):
+        return ref.at[pl.ds(pl.multiple_of(s * piece, piece), piece)]
+
+    scattered, gathered = [], []
+    for d in range(1, n_seq):
+        to = lax.rem(seq + d, n_seq)
+        copy = pltpu.make_async_remote_copy(
+            src_ref=piece_of(state, to), dst_ref=pieces.at[d - 1],
+            send_sem=send_sems.at[len(sends) + d - 1], recv_sem=piece_sems.at[d - 1],
+            device_id={"img": img, "seq": to}, device_id_type=pl.DeviceIdType.MESH,
+        )
+        copy.start()
+        scattered.append(copy)
+    summed = state[pl.ds(pl.multiple_of(seq * piece, piece), piece), :]
+    for d in range(1, n_seq):
+        scattered[d - 1].wait_recv()
+        summed = summed + pieces[d - 1]
+    total[pl.ds(pl.multiple_of(seq * piece, piece), piece), :] = summed
+    for d in range(1, n_seq):
+        copy = pltpu.make_async_remote_copy(
+            src_ref=piece_of(total, seq), dst_ref=piece_of(total, seq),
+            send_sem=send_sems.at[len(sends) + n_seq - 1 + d - 1], recv_sem=total_sems.at[d - 1],
+            device_id={"img": img, "seq": lax.rem(seq + d, n_seq)}, device_id_type=pl.DeviceIdType.MESH,
+        )
+        copy.start()
+        gathered.append(copy)
+    for d in range(1, n_seq):
+        block = piece_of(total, lax.rem(seq + n_seq - d, n_seq))
+        pltpu.make_async_remote_copy(
+            src_ref=block, dst_ref=block, send_sem=send_sems.at[0], recv_sem=total_sems.at[d - 1],
+            device_id={"img": img, "seq": twin}, device_id_type=pl.DeviceIdType.MESH,
+        ).wait_recv()
+
+    for g in range(groups):
+        queries = jax.nn.relu(full[:, LANES * g : LANES * (g + 1)])
+        compact = total[HDIM * g : HDIM * (g + 1), :]
+        outer = jnp.concatenate([compact] * (LANES // HDIM), axis=0) * same
+        key_total = total[HDIM * groups + g : HDIM * groups + g + 1, :]
+        numerator = jnp.dot(queries, outer, precision=HIGHEST, preferred_element_type=jnp.float32)
+        denominator = jnp.dot(
+            queries * key_total, same, precision=HIGHEST, preferred_element_type=jnp.float32
+        )
+        out_ref[:, LANES * g : LANES * (g + 1)] = (
+            numerator / (denominator + attn_eps) * live
+        ).astype(out_ref.dtype)
+
+    for copy in sends + scattered + gathered:
+        copy.wait_send()
+
+
+def fast_body(mesh, tokens, norm_gain, caption, null_caption, keep, bucket_rows, w_qkv):
+    n_img, n_seq = mesh.shape["img"], mesh.shape["seq"]
+    _, grid_rows, grid_cols, features = tokens.shape
+    depth, width = w_qkv.shape
+    inner = width * n_seq // 3
+    token_count = grid_rows * grid_cols
+    n_z = n_seq // 2
+    tail = width % LANES
+    deep_tiles = -(-depth // LANES)
+    packed = depth * (width // LANES) + tail * deep_tiles
+    state_rows = (HDIM + 1) * (inner // LANES)
+    piece = -(-state_rows // (8 * n_seq)) * 8
+    dims = (n_img, n_seq, grid_rows, grid_cols, depth, width, inner)
+    vmem = pl.BlockSpec(memory_space=pltpu.VMEM)
+    smem = pl.BlockSpec(memory_space=pltpu.SMEM)
+    dma = pltpu.SemaphoreType.DMA
+    out = pl.pallas_call(
+        functools.partial(kernel, dims),
+        out_shape=jax.ShapeDtypeStruct((token_count, inner), jnp.bfloat16),
+        in_specs=[vmem, vmem, vmem, vmem, smem, smem, vmem],
+        out_specs=vmem,
+        scratch_shapes=[
+            pltpu.VMEM((packed, LANES), jnp.bfloat16),
+            pltpu.VMEM((n_img, n_seq, packed, LANES), jnp.bfloat16),
+            pltpu.VMEM((n_img, token_count, deep_tiles * LANES), jnp.bfloat16),
+            pltpu.VMEM((n_seq, token_count, -(-width // LANES) * LANES), jnp.float32),
+            pltpu.VMEM((token_count, 3 * inner), jnp.float32),
+            pltpu.VMEM((piece * n_seq, LANES), jnp.float32),
+            pltpu.VMEM((n_seq - 1, piece, LANES), jnp.float32),
+            pltpu.VMEM((piece * n_seq, LANES), jnp.float32),
+            dma((96,)),
+            dma((n_z - 1, PARTS)),
+            dma((n_z, PARTS)),
+            dma((n_z, PARTS)),
+            dma((n_z, PARTS)),
+            dma((n_z, 4, PARTS)),
+            dma((n_seq - 1,)),
+            dma((n_seq - 1,)),
+            dma(()),
+        ],
+        compiler_params=pltpu.CompilerParams(
+            collective_id=0, has_side_effects=True, vmem_limit_bytes=56 * 1024 * 1024
+        ),
+        cost_estimate=pl.CostEstimate(
+            flops=2 * token_count * features * 3 * inner, bytes_accessed=4 * token_count * features,
+            transcendentals=0,
+        ),
+    )(
+        tokens.reshape(token_count, features), norm_gain.reshape(1, features), caption,
+        null_caption.reshape(1, features), keep, bucket_rows, w_qkv,
+    )
+    return out.reshape(1, grid_rows, grid_cols, inner)
 
 
 def body(tokens, norm_gain, caption, null_caption, keep, bucket_rows, w_qkv):
@@ -59,4 +368,6 @@
         P("img", "seq"),
     )
     out_specs = P("img", "seq", None, None)
-    return jax.shard_map(body, mesh=mesh, in_specs=in_specs, out_specs=out_specs, check_vma=False)
+    plane = mesh.shape["img"] == 4 and mesh.shape["seq"] == 8
+    run = functools.partial(fast_body, mesh) if plane else body
+    return jax.shard_map(run, mesh=mesh, in_specs=in_specs, out_specs=out_specs, check_vma=False)

time: 313 us -> 118 us (0.38)
  waiting for transfers between devices: 228 us -> 0 us
  Pallas kernels: 0 us -> 106 us
  blocking collectives: 27.3 us -> 0 us
  matrix products: 19.4 us -> 0 us
  between operations: 14.5 us -> 1.31 us
  other arithmetic: 7.35 us -> 0 us
  local copies, waits for them, and re-layouts: 15.9 us -> 10.7 us
    all_gather x2 -> x0, waiting for transfers between devices: 175 us -> none  [the longest x1 135 us: body(): lax.all_gather(rows_whole, 'seq', axis=1, tiled=True)]
    pallas_call x0 -> x1, Pallas kernels: none -> 106 us  [fast_body(): pl.pallas_call(functools.partial(kernel, dims), out_shape=jax.ShapeDtypeS...]
    psum x1 -> x0, waiting for transfers between devices: 52.3 us -> none  [body(): state_outer, key_total = lax.psum((state_outer, key_total), 'seq')]
    psum x1 -> x0, blocking collectives: 27.3 us -> none  [body(): state_outer, key_total = lax.psum((state_outer, key_total), 'seq')]
    dot_general x4 -> x0, matrix products: 19.4 us -> none  [the longest x1 10.8 us: body(): jnp.dot(hidden, lax.all_gather(rows_whole, 'seq', axis=1, tiled=True), pr...]
    unnamed x5 -> x3, local copies, waits for them, and re-layouts: 2.73 us -> 8.08 us
    convert_element_type x3 -> x0, local copies, waits for them, and re-layouts: 4.85 us -> none  [the longest x1 2.61 us: body(): features = tokens.reshape(token_count, features_count).astype(jnp.float32)]
    max x2 -> x0, local copies, waits for them, and re-layouts: 3.96 us -> none  [the longest x1 2.2 us: body(): jax.nn.relu(projected[:, inner_width:2 * inner_width])]
  transfers between devices with their start and end apart: 3 -> 0, of which waited for: 3 -> 0; matrix products, arithmetic and copies ran while one was open for 4% -> 0% of each run, Pallas kernels for 0% -> 0%
where the time goes in v1:
time: 118 us
  Pallas kernels  106 us (90%)
  local copies, waits for them, and re-layouts  10.7 us (9%)
  between operations  1.31 us (1%)
    pallas_call x1, Pallas kernels, fast_body(): pl.pallas_call(functools.partial(kernel, dims), out_shape=jax.ShapeDtypeS...  106 us
    unnamed x3, local copies, waits for them, and re-layouts  8.08 us

profile of v1, /device:TPU:0, one launch (start us, length us, event | category | flops | bytes accessed | tf_op | source)
XLA Modules:
  0.0 117.7 jit_solution(14263779338857882572)
XLA Ops:
  1.3 1.3 %reshape.13.gain_ref = bf16[1,2240]{1,0:T(2,128)(2,1)} reshape(bf16[2240]{0:T(1024)(128)(2,1)} %param.8) | data formatting | bytes 8960 | tf_op jit(solution)/shard_map/reshape | solution.py:316
  2.6 1.3 %reshape.14.null_ref = bf16[1,2240]{1,0:T(2,128)(2,1)} reshape(bf16[2240]{0:T(1024)(128)(2,1)} %param.10) | data formatting | bytes 8960 | tf_op jit(solution)/shard_map/reshape | solution.py:317
  3.9 2.1 %copy.9.w_ref = bf16[560,432]{1,0:T(8,128)(2,1)} copy(bf16[560,432]{0,1:T(8,128)(2,1)} %param.13) | data formatting | bytes 967680 | tf_op args[6]
  6.0 3.9 %copy.8 = bf16[1,3,128,2240]{3,2,1,0:T(8,128)(2,1)} copy(bf16[1,3,128,2240]{2,3,1,0:T(8,128)(2,1)} %param.7) | data formatting | bytes 3440640 | tf_op args[0]
  9.8 105.7 %shard_map.73 = bf16[384,1152]{1,0:T(8,128)(2,1)} custom-call(bf16[384,2240]{1,0:T(8,128)(2,1)} %bitcast.2, bf16[1,2240]{1,0:T(2,128)(2,1)} %reshape.13.gain_ref, bf16[1,2240]{1,0:T(2,128)(2,1)} %caption_ref.1, bf16[1,2240]{1,0:T(2,128)(2,1)} %reshape.14.null_ref, s32[1]{0:T(128)S(6)} %copy.11.keep_ref, s32[1]{0:T(128)S(6)} %copy.12.rows_ref, ...), custom_call_target="tpu_custom_call" | custom-call | flops 5945425920 | bytes 3440640 | tf_op jit(solution)/shard_map/pallas_call | solution.py:284
  115.5 2.1 %copy.13 = bf16[1,3,128,1152]{3,2,1,0:T(8,128)(2,1)} copy(bf16[1,3,128,1152]{3,2,1,0:T(8,128)(2,1)} %bitcast.3) | data formatting | bytes 1769472

commit v2 on v1

--- a/solution.py
+++ b/solution.py
@@ -13,25 +13,42 @@
 
 norm_eps = 1e-06
 attn_eps = 1e-06
-HIGHEST = lax.Precision.HIGHEST
 
 
 def gray(r):
     return r + r // 2 - 2 * (r // 3)
 
 
+def half_rows(width):
+    return -(-width // 32) * 16
+
+
+def product(a, b, dims):
+    a_high, b_high = a.astype(jnp.bfloat16), b.astype(jnp.bfloat16)
+    a_low = (a - a_high.astype(jnp.float32)).astype(jnp.bfloat16)
+    b_low = (b - b_high.astype(jnp.float32)).astype(jnp.bfloat16)
+    rows = a.shape[0]
+    first = lax.dot_general(
+        jnp.concatenate([a_high, a_low], axis=0), b_high, dims, preferred_element_type=jnp.float32
+    )
+    return (
+        first[0:rows] + first[rows:]
+        + lax.dot_general(a_high, b_low, dims, preferred_element_type=jnp.float32)
+    )
+
+
 def kernel(
     dims,
-    tokens_ref, gain_ref, caption_ref, null_ref, keep_ref, rows_ref, w_ref,
+    tokens_ref, vectors_ref, keep_ref, rows_ref, w_ref,
     out_ref,
-    own, wbuf, hid, proj, full, state, pieces, total,
+    own, wbuf, hid, ends_upper, ends_lower, spread, full, state, pieces, total,
     send_sems, z_sems, left_sems, right_sems, far_sems, twin_sems, piece_sems, total_sems, local_sem,
 ):
     n_img, n_seq, grid_rows, grid_cols, depth, width, inner = dims
-    main_tiles = width // LANES
+    main_tiles = depth // LANES
     main = main_tiles * LANES
-    tail = width - main
-    deep_tiles = -(-depth // LANES)
+    tail = depth - main
+    top = half_rows(width)
     packed = own.shape[0]
     part_rows = packed // PARTS
     n_z = n_seq // 2
@@ -58,19 +75,21 @@
         )
 
     for j in range(main_tiles):
-        own[depth * j : depth * (j + 1), :] = w_ref[:, LANES * j : LANES * (j + 1)]
-    rows_at = lax.broadcasted_iota(jnp.int32, (tail, tail), 0)
-    cols_at = lax.broadcasted_iota(jnp.int32, (tail, tail), 1)
-    unit = (rows_at == cols_at).astype(jnp.bfloat16)
-    rest = lax.dot_general(
-        unit, w_ref[:, main:width], (((1,), (1,)), ((), ())), preferred_element_type=jnp.float32
-    ).astype(jnp.bfloat16)
-    base = depth * main_tiles
-    for j in range(deep_tiles):
-        lanes = min(LANES, depth - LANES * j)
-        if lanes < LANES:
-            own[base + tail * j : base + tail * (j + 1), :] = jnp.zeros((tail, LANES), jnp.bfloat16)
-        own[base + tail * j : base + tail * (j + 1), 0:lanes] = rest[:, LANES * j : LANES * j + lanes]
+        own[width * j : width * (j + 1), :] = w_ref[:, LANES * j : LANES * (j + 1)]
+    rows_at = lax.broadcasted_iota(jnp.int32, (tail, LANES), 0)
+    cols_at = lax.broadcasted_iota(jnp.int32, (tail, LANES), 1)
+    base = width * main_tiles
+    upper = jnp.dot(
+        w_ref[0:top, main:depth], (rows_at == cols_at).astype(jnp.bfloat16),
+        preferred_element_type=jnp.float32,
+    )
+    lower = jnp.dot(
+        w_ref[top:width, main:depth], (rows_at + LANES // 2 == cols_at).astype(jnp.bfloat16),
+        preferred_element_type=jnp.float32,
+    )
+    own[base : base + width - top, :] = (upper[0 : width - top] + lower).astype(jnp.bfloat16)
+    if 2 * top > width:
+        own[base + width - top : base + top, :] = upper[width - top : top].astype(jnp.bfloat16)
 
     pl.semaphore_wait(barrier, len(peers))
 
@@ -111,49 +130,47 @@
         for p in range(PARTS):
             send(own.at[part(p)], img, seq, p, z_sems.at[k - 1, p], img, mine[k])
 
-    keep_flag = (keep_ref[0] > 0).astype(jnp.float32)
-    condition = jnp.where(
-        jnp.full((1, depth * n_img), keep_flag) > 0.5,
-        caption_ref[...].astype(jnp.float32),
-        null_ref[...].astype(jnp.float32),
-    )
-    gain = gain_ref[...].astype(jnp.float32)
-    deep = deep_tiles * LANES
-    if deep > depth:
-        hid[:, :, deep - LANES :] = jnp.zeros((n_img, token_count, LANES), jnp.bfloat16)
-    step_rows = 32
-
-    @pl.loop(0, token_count // step_rows)
-    def _(t):
-        rows = pl.ds(pl.multiple_of(t * step_rows, step_rows), step_rows)
-        features = tokens_ref[rows, :].astype(jnp.float32)
-        mean_square = jnp.mean(features * features, axis=1, keepdims=True)
-        hidden = (features * lax.rsqrt(mean_square + norm_eps) * gain + condition).astype(jnp.bfloat16)
+    flag = jnp.full((1, depth * n_img), keep_ref[0])
+    condition = jnp.where(flag > 0, vectors_ref[1:2, :].astype(jnp.float32), vectors_ref[2:3, :].astype(jnp.float32))
+    pair = jnp.concatenate([vectors_ref[0:1, :].astype(jnp.float32), condition], axis=0).astype(jnp.bfloat16)
+    row_is = lax.broadcasted_iota(jnp.int32, (2, 2 * LANES), 0)
+    col_is = lax.broadcasted_iota(jnp.int32, (2, 2 * LANES), 1) // LANES
+    spread[...] = lax.dot_general(
+        pair, (row_is == col_is).astype(jnp.bfloat16), (((0,), (0,)), ((), ())),
+        preferred_element_type=jnp.float32,
+    )
+    ends_upper[...] = jnp.zeros_like(ends_upper)
+    ends_lower[...] = jnp.zeros_like(ends_lower)
+    for t in range(grid_rows):
+        cols = slice(grid_cols * t, grid_cols * (t + 1))
+        features = tokens_ref[t].astype(jnp.float32)
+        mean_square = jnp.mean(features * features, axis=0, keepdims=True)
+        scale = lax.rsqrt(mean_square + norm_eps)
         for i in range(n_img):
-            hid[i, rows, 0:depth] = hidden[:, depth * i : depth * (i + 1)]
+            rows = slice(depth * i, depth * (i + 1))
+            hidden = (
+                tokens_ref[t, rows, :].astype(jnp.float32) * scale * spread[rows, 0:LANES]
+                + spread[rows, LANES:]
+            ).astype(jnp.bfloat16)
+            hid[main * i : main * (i + 1), cols] = hidden[0:main]
+            ends_upper[LANES * i : LANES * i + tail, cols] = hidden[main:depth]
+            half = LANES * i + LANES // 2
+            ends_lower[half : half + tail, cols] = hidden[main:depth]
 
     keep_own.wait()
 
     def project(s):
-        @pl.loop(0, grid_rows)
-        def _(t):
-            rows = pl.ds(pl.multiple_of(t * grid_cols, grid_cols), grid_cols)
-            acc = jnp.zeros((grid_cols, main), jnp.float32)
-            acc_tail = jnp.zeros((grid_cols, tail), jnp.float32)
-            for i in range(n_img):
-                block = jnp.concatenate(
-                    [wbuf[i, s, depth * j : depth * (j + 1), :] for j in range(main_tiles)], axis=1
-                )
-                acc += jnp.dot(hid[i, rows, 0:depth], block, preferred_element_type=jnp.float32)
-                ends = jnp.concatenate(
-                    [wbuf[i, s, base + tail * j : base + tail * (j + 1), :] for j in range(deep_tiles)],
-                    axis=1,
-                )
-                acc_tail += lax.dot_general(
-                    hid[i, rows, :], ends, (((1,), (1,)), ((), ())), preferred_element_type=jnp.float32
-                )
-            proj[s, rows, 0:main] = acc
-            proj[s, rows, main:width] = acc_tail
+        block = jnp.concatenate(
+            [wbuf[i, s, width * j : width * (j + 1), :] for i in range(n_img) for j in range(main_tiles)],
+            axis=1,
+        )
+        ends = jnp.concatenate([wbuf[i, s, base : base + top, :] for i in range(n_img)], axis=1)
+        acc = jnp.dot(block, hid[...], preferred_element_type=jnp.float32)
+        acc_upper = jnp.dot(ends, ends_upper[...], preferred_element_type=jnp.float32)
+        acc_lower = jnp.dot(ends[0 : width - top], ends_lower[...], preferred_element_type=jnp.float32)
+        at = pl.multiple_of(s * width, width)
+        full[pl.ds(at, top), :] = acc[0:top] + acc_upper
+        full[pl.ds(at + top, width - top), :] = acc[top:width] + acc_lower
 
     def finish(k):
         for p in range(PARTS):
@@ -189,29 +206,23 @@
             send(src, far, s, p, twin_sems.at[k, 3, p], img, twin)
     finish(n_z - 1)
 
-    @pl.loop(0, grid_rows)
-    def _(t):
-        rows = pl.ds(pl.multiple_of(t * grid_cols, grid_cols), grid_cols)
-        for s in range(n_seq):
-            full[rows, width * s : width * (s + 1)] = proj[s, rows, 0:width]
-
     groups = inner // LANES
     head_of_row = lax.broadcasted_iota(jnp.int32, (LANES, LANES), 0) // HDIM
     head_of_col = lax.broadcasted_iota(jnp.int32, (LANES, LANES), 1) // HDIM
     same = (head_of_row == head_of_col).astype(jnp.float32)
-    live_rows = seq * grid_rows + lax.broadcasted_iota(jnp.int32, (token_count, LANES), 0) // grid_cols
+    live_rows = seq * grid_rows + lax.broadcasted_iota(jnp.int32, (1, token_count), 1) // grid_cols
     live = (live_rows < rows_ref[0]).astype(jnp.float32)
     state[...] = jnp.zeros_like(state)
+    by_lanes = (((1,), (1,)), ((), ()))
+    by_rows = (((1,), (0,)), ((), ()))
+    ones = jnp.ones((8, token_count), jnp.float32)
     for g in range(groups):
-        keys = jax.nn.relu(full[:, inner + LANES * g : inner + LANES * (g + 1)]) * live
-        values = full[:, 2 * inner + LANES * g : 2 * inner + LANES * (g + 1)]
-        outer = lax.dot_general(
-            keys, values, (((0,), (0,)), ((), ())), precision=HIGHEST, preferred_element_type=jnp.float32
-        ) * same
-        state[HDIM * g : HDIM * (g + 1), :] = (
-            outer[0:32] + outer[32:64] + outer[64:96] + outer[96:128]
-        )
-        state[HDIM * groups + g : HDIM * groups + g + 1, :] = jnp.sum(keys, axis=0, keepdims=True)
+        keys = jax.nn.relu(full[inner + LANES * g : inner + LANES * (g + 1), :]) * live
+        values = full[2 * inner + LANES * g : 2 * inner + LANES * (g + 1), :]
+        outer = product(jnp.concatenate([values, ones], axis=0), keys, by_lanes)
+        kept = outer[0:LANES] * same
+        state[HDIM * g : HDIM * (g + 1), :] = kept[0:32] + kept[32:64] + kept[64:96] + kept[96:128]
+        state[HDIM * groups + g : HDIM * groups + g + 1, :] = outer[LANES : LANES + 1]
 
     piece = state.shape[0] // n_seq
 
@@ -249,17 +260,14 @@
         ).wait_recv()
 
     for g in range(groups):
-        queries = jax.nn.relu(full[:, LANES * g : LANES * (g + 1)])
+        queries = jax.nn.relu(full[LANES * g : LANES * (g + 1), :])
         compact = total[HDIM * g : HDIM * (g + 1), :]
         outer = jnp.concatenate([compact] * (LANES // HDIM), axis=0) * same
-        key_total = total[HDIM * groups + g : HDIM * groups + g + 1, :]
-        numerator = jnp.dot(queries, outer, precision=HIGHEST, preferred_element_type=jnp.float32)
-        denominator = jnp.dot(
-            queries * key_total, same, precision=HIGHEST, preferred_element_type=jnp.float32
-        )
-        out_ref[:, LANES * g : LANES * (g + 1)] = (
-            numerator / (denominator + attn_eps) * live
-        ).astype(out_ref.dtype)
+        key_total = total[HDIM * groups + g : HDIM * groups + g + 1, :] * same
+        both = product(jnp.concatenate([outer, key_total], axis=0), queries, by_rows)
+        result = (both[0:LANES] / (both[LANES:] + attn_eps) * live).astype(out_ref.dtype)
+        for t in range(grid_rows):
+            out_ref[t, LANES * g : LANES * (g + 1), :] = result[:, grid_cols * t : grid_cols * (t + 1)]
 
     for copy in sends + scattered + gathered:
         copy.wait_send()
@@ -272,9 +280,7 @@
     inner = width * n_seq // 3
     token_count = grid_rows * grid_cols
     n_z = n_seq // 2
-    tail = width % LANES
-    deep_tiles = -(-depth // LANES)
-    packed = depth * (width // LANES) + tail * deep_tiles
+    packed = width * (depth // LANES) + half_rows(width)
     state_rows = (HDIM + 1) * (inner // LANES)
     piece = -(-state_rows // (8 * n_seq)) * 8
     dims = (n_img, n_seq, grid_rows, grid_cols, depth, width, inner)
@@ -283,15 +289,17 @@
     dma = pltpu.SemaphoreType.DMA
     out = pl.pallas_call(
         functools.partial(kernel, dims),
-        out_shape=jax.ShapeDtypeStruct((token_count, inner), jnp.bfloat16),
-        in_specs=[vmem, vmem, vmem, vmem, smem, smem, vmem],
+        out_shape=jax.ShapeDtypeStruct((grid_rows, inner, grid_cols), jnp.bfloat16),
+        in_specs=[vmem, vmem, smem, smem, vmem],
         out_specs=vmem,
         scratch_shapes=[
             pltpu.VMEM((packed, LANES), jnp.bfloat16),
             pltpu.VMEM((n_img, n_seq, packed, LANES), jnp.bfloat16),
-            pltpu.VMEM((n_img, token_count, deep_tiles * LANES), jnp.bfloat16),
-            pltpu.VMEM((n_seq, token_count, -(-width // LANES) * LANES), jnp.float32),
-            pltpu.VMEM((token_count, 3 * inner), jnp.float32),
+            pltpu.VMEM((n_img * (depth // LANES) * LANES, token_count), jnp.bfloat16),
+            pltpu.VMEM((n_img * LANES, token_count), jnp.bfloat16),
+            pltpu.VMEM((n_img * LANES, token_count), jnp.bfloat16),
+            pltpu.VMEM((features, 2 * LANES), jnp.float32),
+            pltpu.VMEM((3 * inner, token_count), jnp.float32),
             pltpu.VMEM((piece * n_seq, LANES), jnp.float32),
             pltpu.VMEM((n_seq - 1, piece, LANES), jnp.float32),
             pltpu.VMEM((piece * n_seq, LANES), jnp.float32),
@@ -313,10 +321,10 @@
             transcendentals=0,
         ),
     )(
-        tokens.reshape(token_count, features), norm_gain.reshape(1, features), caption,
-        null_caption.reshape(1, features), keep, bucket_rows, w_qkv,
-    )
-    return out.reshape(1, grid_rows, grid_cols, inner)
+        tokens.transpose(0, 1, 3, 2).reshape(grid_rows, features, grid_cols),
+        jnp.stack([norm_gain, caption[0], null_caption]), keep, bucket_rows, w_qkv.T,
+    )
+    return out.transpose(0, 2, 1).reshape(1, grid_rows, grid_cols, inner)
 
 
 def body(tokens, norm_gain, caption, null_caption, keep, bucket_rows, w_qkv):

time: 118 us -> 107 us (0.907)
  local copies, waits for them, and re-layouts: 10.7 us -> 3.62 us
  Pallas kernels: 106 us -> 101 us
  other arithmetic: 0 us -> 1.34 us
    unnamed x3 -> x0, local copies, waits for them, and re-layouts: 8.08 us -> none
    pallas_call x1, Pallas kernels: 106 us -> 101 us  [fast_body(): pl.pallas_call(functools.partial(kernel, dims), out_shape=jax.ShapeDtypeS...]
    another operation x0 -> x2, local copies, waits for them, and re-layouts: none -> 1.4 us  [fast_body(): jnp.stack([norm_gain, caption[0], null_caption])]
    another operation x0 -> x1, other arithmetic: none -> 1.34 us  [fast_body(): jnp.stack([norm_gain, caption[0], null_caption])]
    reshape x2 -> x1, local copies, waits for them, and re-layouts: 2.58 us -> 2.22 us  [fast_body(): return out.transpose(0, 2, 1).reshape(1, grid_rows, grid_cols, inner)]
where the time goes in v2:
time: 107 us
  Pallas kernels  101 us (94%)
  local copies, waits for them, and re-layouts  3.62 us (3%)
  other arithmetic  1.34 us (1%)
  between operations  1.31 us (1%)
    pallas_call x1, Pallas kernels, fast_body(): pl.pallas_call(functools.partial(kernel, dims), out_shape=jax.ShapeDtypeS...  101 us
    reshape x1, local copies, waits for them, and re-layouts, fast_body(): return out.transpose(0, 2, 1).reshape(1, grid_rows, grid_cols, inner)  2.22 us

profile of v2, /device:TPU:0, one launch (start us, length us, event | category | flops | bytes accessed | tf_op | source)
XLA Modules:
  0.0 107.1 jit_solution(14840003792161862987)
XLA Ops:
  1.3 0.7 stack.9
  2.0 0.7 stack.10
  2.7 1.3 %pad_maximum_fusion.vectors_ref = bf16[3,2240]{1,0:T(4,128)(2,1)} fusion(bf16[1,2240]{1,0:T(2,128)(2,1)S(1)} %stack.10, bf16[1,2240]{1,0:T(2,128)(2,1)} %param.9, bf16[1,2240]{1,0:T(2,128)(2,1)S(1)} %stack.9), kind=kLoop, calls=%fused_computation | loop fusion | flops 40320 | bytes 26880 | tf_op jit(solution)/shard_map/stack | solution.py:325
  4.0 100.8 %shard_map.73 = bf16[3,1152,128]{2,1,0:T(8,128)(2,1)} custom-call(bf16[3,2240,128]{2,1,0:T(8,128)(2,1)} %bitcast.8, bf16[3,2240]{1,0:T(4,128)(2,1)} %pad_maximum_fusion.vectors_ref, s32[1]{0:T(128)S(6)} %copy.9.keep_ref, s32[1]{0:T(128)S(6)} %copy.10.rows_ref, bf16[432,560]{1,0:T(8,128)(2,1)} %bitcast.9), custom_call_target="tpu_custom_call" | custom-call | flops 5945425920 | bytes 3440640 | tf_op jit(solution)/shard_map/pallas_call | solution.py:290
  104.8 2.2 %copy.8 = bf16[1,3,128,1152]{3,2,1,0:T(8,128)(2,1)} copy(bf16[1,3,128,1152]{2,3,1,0:T(8,128)(2,1)} %bitcast.7) | data formatting | bytes 1769472 | tf_op jit(solution)/shard_map/reshape | solution.py:327

commit v3 on v2

--- a/solution.py
+++ b/solution.py
@@ -9,7 +9,6 @@
 
 HDIM = 32
 LANES = 128
-PARTS = 2
 
 norm_eps = 1e-06
 attn_eps = 1e-06
@@ -21,6 +20,19 @@
 
 def half_rows(width):
     return -(-width // 32) * 16
+
+
+def parts_of(packed):
+    units = packed // 16
+    b = round(units * 2 / 9)
+    a = units - b
+    cuts = [0, (a + 1) // 2, a, a + (b + 1) // 2, units]
+    cuts = [16 * c for c in cuts]
+
+    def span(i, j):
+        return (cuts[i], cuts[j] - cuts[i])
+
+    return span(0, 2), span(0, 1), span(1, 2), span(2, 4), span(2, 3), span(3, 4)
 
 
 def product(a, b, dims):
@@ -42,7 +54,7 @@
     tokens_ref, vectors_ref, keep_ref, rows_ref, w_ref,
     out_ref,
     own, wbuf, hid, ends_upper, ends_lower, spread, full, state, pieces, total,
-    send_sems, z_sems, left_sems, right_sems, far_sems, twin_sems, piece_sems, total_sems, local_sem,
+    send_sems, in_sems, twin_sems, piece_sems, total_sems, local_sem,
 ):
     n_img, n_seq, grid_rows, grid_cols, depth, width, inner = dims
     main_tiles = depth // LANES
@@ -50,7 +62,7 @@
     tail = depth - main
     top = half_rows(width)
     packed = own.shape[0]
-    part_rows = packed // PARTS
+    A, A0, A1, B, B0, B1 = parts_of(packed)
     n_z = n_seq // 2
     token_count = grid_rows * grid_cols
 
@@ -63,7 +75,7 @@
     left = gray(lax.rem(ring + 3, 4))
     far = gray(lax.rem(ring + 2, 4))
     twin = seq + 1 - 2 * core
-    zs = [z, z + 1 - 2 * lax.rem(z, 2), lax.rem(z + 2, 4), 3 - z]
+    zs = [z, z + 1 - 2 * lax.rem(z, 2), 2 - z // 2, 3 - 3 * (z // 2)]
     mine = [2 * q + core for q in zs]
     twins = [2 * q + 1 - core for q in zs]
 
@@ -95,40 +107,69 @@
 
     sends = []
 
-    def part(p):
-        return pl.ds(p * part_rows, part_rows)
-
-    def send(src, i, s, p, recv_sem, to_img, to_seq):
+    def send(src, i, s, span, recv_sem, to_img, to_seq, when=None):
         copy = pltpu.make_async_remote_copy(
-            src_ref=src,
-            dst_ref=wbuf.at[i, s, part(p)],
+            src_ref=src.at[pl.ds(*span)],
+            dst_ref=wbuf.at[i, s, pl.ds(*span)],
             send_sem=send_sems.at[len(sends)],
             recv_sem=recv_sem,
             device_id={"img": to_img, "seq": to_seq},
             device_id_type=pl.DeviceIdType.MESH,
         )
-        copy.start()
-        sends.append(copy)
-
-    def arrive(i, s, p, recv_sem):
-        block = wbuf.at[i, s, part(p)]
+        if when is None:
+            copy.start()
+        else:
+            pl.when(when)(copy.start)
+        sends.append((copy, when))
+
+    def arrive(i, s, span, recv_sem):
+        block = wbuf.at[i, s, pl.ds(*span)]
         pltpu.make_async_remote_copy(
             src_ref=block, dst_ref=block, send_sem=send_sems.at[0], recv_sem=recv_sem,
             device_id={"img": img, "seq": twin}, device_id_type=pl.DeviceIdType.MESH,
         ).wait_recv()
-        return block
+
+    slot = {A0: 0, A1: 1, B0: 2, B1: 3, B: 2}
+
+    def get(i, q, *spans):
+        for span in spans:
+            arrive(i, 2 * q + core, span, in_sems.at[i, q, slot[span]])
+
+    def give(src, i, q, to, *spans):
+        for span in spans:
+            send(src, i, 2 * q + core, span, in_sems.at[i, q, slot[span]], to, seq)
+
+    def share(src, i, q, *spans):
+        for span in spans:
+            send(src, i, 2 * q + core, span, twin_sems.at[i, q, 0 if span == A else 1], img, twin)
+
+    def start_line(src, i, spans):
+        for span in spans:
+            sem = in_sems.at[i, z, slot[span]]
+            send(src, i, seq, span, sem, img, lax.rem(seq + 2, n_seq), z < n_z - 1)
+            send(src, i, seq, span, sem, img, lax.rem(seq + n_seq - 2, n_seq), z > 0)
+
+    def relay(src, i, q, spans):
+        to = z - 1 + 2 * (q < z).astype(jnp.int32)
+        inside = jnp.logical_and(to >= 0, to < n_z)
+        to_seq = lax.rem(2 * to + core + n_seq, n_seq)
+        for span in spans:
+            send(src, i, 2 * q + core, span, in_sems.at[i, q, slot[span]], img, to_seq, inside)
+
+    def block_of(i, q):
+        return wbuf.at[i, 2 * q + core]
 
     keep_own = pltpu.make_async_copy(own, wbuf.at[img, seq], local_sem)
     keep_own.start()
-    for p in range(PARTS):
-        src = own.at[part(p)]
-        send(src, img, seq, p, left_sems.at[0, p], right, seq)
-        send(src, img, seq, p, right_sems.at[0, p], left, seq)
-        send(src, img, seq, p, z_sems.at[0, p], img, mine[1])
-        send(src, img, seq, p, twin_sems.at[0, 0, p], img, twin)
-    for k in range(2, n_z):
-        for p in range(PARTS):
-            send(own.at[part(p)], img, seq, p, z_sems.at[k - 1, p], img, mine[k])
+    for span in (A0, A1):
+        give(own, img, z, right, span)
+        give(own, img, z, left, span)
+        start_line(own, img, [span])
+    for span in (B0, B1):
+        give(own, img, z, right, span)
+        give(own, img, z, left, span)
+    start_line(own, img, [B])
+    share(own, img, z, A, B)
 
     flag = jnp.full((1, depth * n_img), keep_ref[0])
     condition = jnp.where(flag > 0, vectors_ref[1:2, :].astype(jnp.float32), vectors_ref[2:3, :].astype(jnp.float32))
@@ -173,37 +214,62 @@
         full[pl.ds(at + top, width - top), :] = acc[top:width] + acc_lower
 
     def finish(k):
-        for p in range(PARTS):
-            for at, i in enumerate((img, left, right)):
-                arrive(i, twins[k], p, twin_sems.at[k, at, p])
-        arrive(far, twins[k], 0, twin_sems.at[k, 3, 0])
-        arrive(far, twins[k], 1, twin_sems.at[k, 3, 1])
+        for i in (img, left, right, far):
+            arrive(i, twins[k], A, twin_sems.at[i, zs[k], 0])
+            arrive(i, twins[k], B, twin_sems.at[i, zs[k], 1])
         project(mine[k])
         project(twins[k])
 
+    def side_rows(q):
+        for i in (left, right, far):
+            get(i, q, B)
+            relay(block_of(i, q), i, q, [B])
+            share(block_of(i, q), i, q, B)
+
     for k in range(n_z):
         if k + 1 < n_z:
-            s = mine[k + 1]
-            for p in range(PARTS):
-                src = arrive(img, s, p, z_sems.at[k, p])
-                send(src, img, s, p, left_sems.at[k + 1, p], right, seq)
-                send(src, img, s, p, right_sems.at[k + 1, p], left, seq)
-                send(src, img, s, p, twin_sems.at[k + 1, 0, p], img, twin)
-        s = mine[k]
-        for p in range(PARTS):
-            src = arrive(left, s, p, left_sems.at[k, p])
-            if p == 0:
-                send(src, left, s, p, far_sems.at[k, 0], right, seq)
-            send(src, left, s, p, twin_sems.at[k, 1, p], img, twin)
-            src = arrive(right, s, p, right_sems.at[k, p])
-            if p == 1:
-                send(src, right, s, p, far_sems.at[k, 1], left, seq)
-            send(src, right, s, p, twin_sems.at[k, 2, p], img, twin)
-        if k > 0:
+            q = zs[k + 1]
+            src = block_of(img, q)
+            for span in (A0, A1):
+                get(img, q, span)
+                give(src, img, q, right, span)
+                give(src, img, q, left, span)
+                relay(src, img, q, [span])
+            get(img, q, B)
+            relay(src, img, q, [B])
+            share(src, img, q, A, B)
+        q = zs[k]
+        from_left, from_right, from_far = block_of(left, q), block_of(right, q), block_of(far, q)
+        get(left, q, A0)
+        give(from_left, left, q, right, A0)
+        get(right, q, A0, A1)
+        give(from_right, right, q, left, A1)
+        share(from_right, right, q, A)
+        get(left, q, A1)
+        share(from_left, left, q, A)
+        if k == 0:
+            get(left, q, B0)
+            give(from_left, left, q, right, B0)
+            get(right, q, B0, B1)
+            give(from_right, right, q, left, B1)
+            start_line(from_right, right, [B])
+            share(from_right, right, q, B)
+            get(left, q, B1)
+            start_line(from_left, left, [B])
+            share(from_left, left, q, B)
+        elif k == 1:
+            side_rows(q)
+        elif k == 2:
+            side_rows(q)
+            side_rows(zs[3])
+        get(far, q, A0, A1)
+        share(from_far, far, q, A)
+        if k == 0:
+            get(far, q, B0, B1)
+            start_line(from_far, far, [B])
+            share(from_far, far, q, B)
+        else:
             finish(k - 1)
-        for p in range(PARTS):
-            src = arrive(far, s, p, far_sems.at[k, p])
-            send(src, far, s, p, twin_sems.at[k, 3, p], img, twin)
     finish(n_z - 1)
 
     groups = inner // LANES
@@ -269,7 +335,12 @@
         for t in range(grid_rows):
             out_ref[t, LANES * g : LANES * (g + 1), :] = result[:, grid_cols * t : grid_cols * (t + 1)]
 
-    for copy in sends + scattered + gathered:
+    for copy, when in sends:
+        if when is None:
+            copy.wait_send()
+        else:
+            pl.when(when)(copy.wait_send)
+    for copy in scattered + gathered:
         copy.wait_send()
 
 
@@ -303,12 +374,9 @@
             pltpu.VMEM((piece * n_seq, LANES), jnp.float32),
             pltpu.VMEM((n_seq - 1, piece, LANES), jnp.float32),
             pltpu.VMEM((piece * n_seq, LANES), jnp.float32),
-            dma((96,)),
-            dma((n_z - 1, PARTS)),
-            dma((n_z, PARTS)),
-            dma((n_z, PARTS)),
-            dma((n_z, PARTS)),
-            dma((n_z, 4, PARTS)),
+            dma((192,)),
+            dma((n_img, n_z, 4)),
+            dma((n_img, n_z, 2)),
             dma((n_seq - 1,)),
             dma((n_seq - 1,)),
             dma(()),

time: 107 us -> 110 us (1.028)
  Pallas kernels: 101 us -> 103 us
    pallas_call x1, Pallas kernels: 101 us -> 103 us  [fast_body(): pl.pallas_call(functools.partial(kernel, dims), out_shape=jax.ShapeDtypeS...]
where the time goes in v3:
time: 110 us
  Pallas kernels  103 us (94%)
  local copies, waits for them, and re-layouts  3.62 us (3%)
  other arithmetic  1.34 us (1%)
  between operations  1.31 us (1%)
    pallas_call x1, Pallas kernels, fast_body(): pl.pallas_call(functools.partial(kernel, dims), out_shape=jax.ShapeDtypeS...  103 us
    reshape x1, local copies, waits for them, and re-layouts, fast_body(): return out.transpose(0, 2, 1).reshape(1, grid_rows, grid_cols, inner)  2.22 us

profile of v3, /device:TPU:0, one launch (start us, length us, event | category | flops | bytes accessed | tf_op | source)
XLA Modules:
  0.0 109.7 jit_solution(13226657576793194522)
XLA Ops:
  1.3 0.7 stack.9
  2.0 0.7 stack.10
  2.7 1.3 %pad_maximum_fusion.vectors_ref = bf16[3,2240]{1,0:T(4,128)(2,1)} fusion(bf16[1,2240]{1,0:T(2,128)(2,1)S(1)} %stack.10, bf16[1,2240]{1,0:T(2,128)(2,1)} %param.9, bf16[1,2240]{1,0:T(2,128)(2,1)S(1)} %stack.9), kind=kLoop, calls=%fused_computation | loop fusion | flops 40320 | bytes 26880 | tf_op jit(solution)/shard_map/stack | solution.py:393
  4.0 103.4 %shard_map.73 = bf16[3,1152,128]{2,1,0:T(8,128)(2,1)} custom-call(bf16[3,2240,128]{2,1,0:T(8,128)(2,1)} %bitcast.8, bf16[3,2240]{1,0:T(4,128)(2,1)} %pad_maximum_fusion.vectors_ref, s32[1]{0:T(128)S(6)} %copy.9.keep_ref, s32[1]{0:T(128)S(6)} %copy.10.rows_ref, bf16[432,560]{1,0:T(8,128)(2,1)} %bitcast.9), custom_call_target="tpu_custom_call" | custom-call | flops 5945425920 | bytes 3440640 | tf_op jit(solution)/shard_map/pallas_call | solution.py:361
  107.5 2.2 %copy.8 = bf16[1,3,128,1152]{3,2,1,0:T(8,128)(2,1)} copy(bf16[1,3,128,1152]{2,3,1,0:T(8,128)(2,1)} %bitcast.7) | data formatting | bytes 1769472 | tf_op jit(solution)/shard_map/reshape | solution.py:395

commit v4 on v3

--- a/solution.py
+++ b/solution.py
@@ -53,8 +53,8 @@
     dims,
     tokens_ref, vectors_ref, keep_ref, rows_ref, w_ref,
     out_ref,
-    own, wbuf, hid, ends_upper, ends_lower, spread, full, state, pieces, total,
-    send_sems, in_sems, twin_sems, piece_sems, total_sems, local_sem,
+    own, wbuf, hid, ends_upper, ends_lower, spread, returns, full, state, pieces, total,
+    send_sems, in_sems, swap_send, swap_recv, piece_sems, total_sems, local_sem,
 ):
     n_img, n_seq, grid_rows, grid_cols, depth, width, inner = dims
     main_tiles = depth // LANES
@@ -107,10 +107,10 @@
 
     sends = []
 
-    def send(src, i, s, span, recv_sem, to_img, to_seq, when=None):
+    def send(src, i, q, span, recv_sem, to_img, to_seq, when=None):
         copy = pltpu.make_async_remote_copy(
             src_ref=src.at[pl.ds(*span)],
-            dst_ref=wbuf.at[i, s, pl.ds(*span)],
+            dst_ref=wbuf.at[i, q, pl.ds(*span)],
             send_sem=send_sems.at[len(sends)],
             recv_sem=recv_sem,
             device_id={"img": to_img, "seq": to_seq},
@@ -122,8 +122,8 @@
             pl.when(when)(copy.start)
         sends.append((copy, when))
 
-    def arrive(i, s, span, recv_sem):
-        block = wbuf.at[i, s, pl.ds(*span)]
+    def arrive(i, q, span, recv_sem):
+        block = wbuf.at[i, q, pl.ds(*span)]
         pltpu.make_async_remote_copy(
             src_ref=block, dst_ref=block, send_sem=send_sems.at[0], recv_sem=recv_sem,
             device_id={"img": img, "seq": twin}, device_id_type=pl.DeviceIdType.MESH,
@@ -133,33 +133,29 @@
 
     def get(i, q, *spans):
         for span in spans:
-            arrive(i, 2 * q + core, span, in_sems.at[i, q, slot[span]])
+            arrive(i, q, span, in_sems.at[i, q, slot[span]])
 
     def give(src, i, q, to, *spans):
         for span in spans:
-            send(src, i, 2 * q + core, span, in_sems.at[i, q, slot[span]], to, seq)
-
-    def share(src, i, q, *spans):
-        for span in spans:
-            send(src, i, 2 * q + core, span, twin_sems.at[i, q, 0 if span == A else 1], img, twin)
+            send(src, i, q, span, in_sems.at[i, q, slot[span]], to, seq)
 
     def start_line(src, i, spans):
         for span in spans:
             sem = in_sems.at[i, z, slot[span]]
-            send(src, i, seq, span, sem, img, lax.rem(seq + 2, n_seq), z < n_z - 1)
-            send(src, i, seq, span, sem, img, lax.rem(seq + n_seq - 2, n_seq), z > 0)
+            send(src, i, z, span, sem, img, lax.rem(seq + 2, n_seq), z < n_z - 1)
+            send(src, i, z, span, sem, img, lax.rem(seq + n_seq - 2, n_seq), z > 0)
 
     def relay(src, i, q, spans):
         to = z - 1 + 2 * (q < z).astype(jnp.int32)
         inside = jnp.logical_and(to >= 0, to < n_z)
         to_seq = lax.rem(2 * to + core + n_seq, n_seq)
         for span in spans:
-            send(src, i, 2 * q + core, span, in_sems.at[i, q, slot[span]], img, to_seq, inside)
+            send(src, i, q, span, in_sems.at[i, q, slot[span]], img, to_seq, inside)
 
     def block_of(i, q):
-        return wbuf.at[i, 2 * q + core]
-
-    keep_own = pltpu.make_async_copy(own, wbuf.at[img, seq], local_sem)
+        return wbuf.at[i, q]
+
+    keep_own = pltpu.make_async_copy(own, wbuf.at[img, z], local_sem)
     keep_own.start()
     for span in (A0, A1):
         give(own, img, z, right, span)
@@ -169,7 +165,6 @@
         give(own, img, z, right, span)
         give(own, img, z, left, span)
     start_line(own, img, [B])
-    share(own, img, z, A, B)
 
     flag = jnp.full((1, depth * n_img), keep_ref[0])
     condition = jnp.where(flag > 0, vectors_ref[1:2, :].astype(jnp.float32), vectors_ref[2:3, :].astype(jnp.float32))
@@ -180,7 +175,7 @@
         pair, (row_is == col_is).astype(jnp.bfloat16), (((0,), (0,)), ((), ())),
         preferred_element_type=jnp.float32,
     )
-    ends_upper[...] = jnp.zeros_like(ends_upper)
+    ends_upper[:, 0:token_count] = jnp.zeros((n_img * LANES, token_count), jnp.bfloat16)
     ends_lower[...] = jnp.zeros_like(ends_lower)
     for t in range(grid_rows):
         cols = slice(grid_cols * t, grid_cols * (t + 1))
@@ -200,31 +195,55 @@
 
     keep_own.wait()
 
-    def project(s):
+    def swap(n, src_ref, dst_ref):
+        return pltpu.make_async_remote_copy(
+            src_ref=src_ref, dst_ref=dst_ref, send_sem=swap_send.at[n], recv_sem=swap_recv.at[n],
+            device_id={"img": img, "seq": twin}, device_id_type=pl.DeviceIdType.MESH,
+        )
+
+    here, there = pl.ds(0, token_count), pl.ds(token_count, token_count)
+    swaps = [swap(0, hid.at[:, here], hid.at[:, there]), swap(1, ends_upper.at[:, here], ends_upper.at[:, there])]
+    for copy in swaps:
+        copy.start()
+
+    def project(k):
         block = jnp.concatenate(
-            [wbuf[i, s, width * j : width * (j + 1), :] for i in range(n_img) for j in range(main_tiles)],
+            [
+                wbuf[i, zs[k], width * j : width * (j + 1), :]
+                for i in range(n_img)
+                for j in range(main_tiles)
+            ],
             axis=1,
         )
-        ends = jnp.concatenate([wbuf[i, s, base : base + top, :] for i in range(n_img)], axis=1)
+        ends = jnp.concatenate([wbuf[i, zs[k], base : base + top, :] for i in range(n_img)], axis=1)
         acc = jnp.dot(block, hid[...], preferred_element_type=jnp.float32)
         acc_upper = jnp.dot(ends, ends_upper[...], preferred_element_type=jnp.float32)
         acc_lower = jnp.dot(ends[0 : width - top], ends_lower[...], preferred_element_type=jnp.float32)
-        at = pl.multiple_of(s * width, width)
-        full[pl.ds(at, top), :] = acc[0:top] + acc_upper
-        full[pl.ds(at + top, width - top), :] = acc[top:width] + acc_lower
+        at = pl.multiple_of(mine[k] * width, width)
+        first, second = acc[0:top] + acc_upper, acc[top:width] + acc_lower
+        returns[k, 0:top, :] = first[:, token_count:]
+        returns[k, top:width, :] = second[:, token_count:]
+        copy = swap(2 + k, returns.at[k], full.at[pl.ds(at, width)])
+        copy.start()
+        swaps.append(copy)
+        full[pl.ds(at, top), :] = first[:, 0:token_count]
+        full[pl.ds(at + top, width - top), :] = second[:, 0:token_count]
 
     def finish(k):
-        for i in (img, left, right, far):
-            arrive(i, twins[k], A, twin_sems.at[i, zs[k], 0])
-            arrive(i, twins[k], B, twin_sems.at[i, zs[k], 1])
-        project(mine[k])
-        project(twins[k])
+        if k == 0:
+            swaps[0].wait_recv()
+            swaps[1].wait_recv()
+            for i in range(n_img):
+                half = LANES * i + LANES // 2
+                ends_lower[half : half + tail, token_count:] = ends_upper[
+                    LANES * i : LANES * i + tail, token_count:
+                ]
+        project(k)
 
     def side_rows(q):
         for i in (left, right, far):
             get(i, q, B)
             relay(block_of(i, q), i, q, [B])
-            share(block_of(i, q), i, q, B)
 
     for k in range(n_z):
         if k + 1 < n_z:
@@ -237,40 +256,37 @@
                 relay(src, img, q, [span])
             get(img, q, B)
             relay(src, img, q, [B])
-            share(src, img, q, A, B)
         q = zs[k]
         from_left, from_right, from_far = block_of(left, q), block_of(right, q), block_of(far, q)
         get(left, q, A0)
         give(from_left, left, q, right, A0)
         get(right, q, A0, A1)
         give(from_right, right, q, left, A1)
-        share(from_right, right, q, A)
         get(left, q, A1)
-        share(from_left, left, q, A)
         if k == 0:
             get(left, q, B0)
             give(from_left, left, q, right, B0)
             get(right, q, B0, B1)
             give(from_right, right, q, left, B1)
             start_line(from_right, right, [B])
-            share(from_right, right, q, B)
             get(left, q, B1)
             start_line(from_left, left, [B])
-            share(from_left, left, q, B)
         elif k == 1:
             side_rows(q)
         elif k == 2:
             side_rows(q)
             side_rows(zs[3])
         get(far, q, A0, A1)
-        share(from_far, far, q, A)
         if k == 0:
             get(far, q, B0, B1)
             start_line(from_far, far, [B])
-            share(from_far, far, q, B)
         else:
             finish(k - 1)
     finish(n_z - 1)
+
+    for k in range(n_z):
+        rows = full.at[pl.ds(pl.multiple_of(twins[k] * width, width), width)]
+        swap(2 + k, rows, rows).wait_recv()
 
     groups = inner // LANES
     head_of_row = lax.broadcasted_iota(jnp.int32, (LANES, LANES), 0) // HDIM
@@ -340,7 +356,7 @@
             copy.wait_send()
         else:
             pl.when(when)(copy.wait_send)
-    for copy in scattered + gathered:
+    for copy in swaps + scattered + gathered:
         copy.wait_send()
 
 
@@ -365,18 +381,20 @@
         out_specs=vmem,
         scratch_shapes=[
             pltpu.VMEM((packed, LANES), jnp.bfloat16),
-            pltpu.VMEM((n_img, n_seq, packed, LANES), jnp.bfloat16),
-            pltpu.VMEM((n_img * (depth // LANES) * LANES, token_count), jnp.bfloat16),
-            pltpu.VMEM((n_img * LANES, token_count), jnp.bfloat16),
-            pltpu.VMEM((n_img * LANES, token_count), jnp.bfloat16),
+            pltpu.VMEM((n_img, n_z, packed, LANES), jnp.bfloat16),
+            pltpu.VMEM((n_img * (depth // LANES) * LANES, 2 * token_count), jnp.bfloat16),
+            pltpu.VMEM((n_img * LANES, 2 * token_count), jnp.bfloat16),
+            pltpu.VMEM((n_img * LANES, 2 * token_count), jnp.bfloat16),
             pltpu.VMEM((features, 2 * LANES), jnp.float32),
+            pltpu.VMEM((n_z, width, token_count), jnp.float32),
             pltpu.VMEM((3 * inner, token_count), jnp.float32),
             pltpu.VMEM((piece * n_seq, LANES), jnp.float32),
             pltpu.VMEM((n_seq - 1, piece, LANES), jnp.float32),
             pltpu.VMEM((piece * n_seq, LANES), jnp.float32),
             dma((192,)),
             dma((n_img, n_z, 4)),
-            dma((n_img, n_z, 2)),
+            dma((2 + n_z,)),
+            dma((2 + n_z,)),
             dma((n_seq - 1,)),
             dma((n_seq - 1,)),
             dma(()),

time: 110 us -> 111 us (level)
  no operation moved by 1% of the time
where the time goes in v4:
time: 111 us
  Pallas kernels  104 us (94%)
  local copies, waits for them, and re-layouts  3.62 us (3%)
  other arithmetic  1.34 us (1%)
  between operations  1.31 us (1%)
    pallas_call x1, Pallas kernels, fast_body(): pl.pallas_call(functools.partial(kernel, dims), out_shape=jax.ShapeDtypeS...  104 us
    reshape x1, local copies, waits for them, and re-layouts, fast_body(): return out.transpose(0, 2, 1).reshape(1, grid_rows, grid_cols, inner)  2.22 us

profile of v4, /device:TPU:0, one launch (start us, length us, event | category | flops | bytes accessed | tf_op | source)
XLA Modules:
  0.0 110.7 jit_solution(11835990542392947441)
XLA Ops:
  1.3 0.7 stack.9
  2.0 0.7 stack.10
  2.7 1.3 %pad_maximum_fusion.vectors_ref = bf16[3,2240]{1,0:T(4,128)(2,1)} fusion(bf16[1,2240]{1,0:T(2,128)(2,1)S(1)} %stack.10, bf16[1,2240]{1,0:T(2,128)(2,1)} %param.9, bf16[1,2240]{1,0:T(2,128)(2,1)S(1)} %stack.9), kind=kLoop, calls=%fused_computation | loop fusion | flops 40320 | bytes 26880 | tf_op jit(solution)/shard_map/stack | solution.py:411
  4.0 104.5 %shard_map.73 = bf16[3,1152,128]{2,1,0:T(8,128)(2,1)} custom-call(bf16[3,2240,128]{2,1,0:T(8,128)(2,1)} %bitcast.8, bf16[3,2240]{1,0:T(4,128)(2,1)} %pad_maximum_fusion.vectors_ref, s32[1]{0:T(128)S(6)} %copy.9.keep_ref, s32[1]{0:T(128)S(6)} %copy.10.rows_ref, bf16[432,560]{1,0:T(8,128)(2,1)} %bitcast.9), custom_call_target="tpu_custom_call" | custom-call | flops 5945425920 | bytes 3440640 | tf_op jit(solution)/shard_map/pallas_call | solution.py:377
  108.5 2.2 %copy.8 = bf16[1,3,128,1152]{3,2,1,0:T(8,128)(2,1)} copy(bf16[1,3,128,1152]{2,3,1,0:T(8,128)(2,1)} %bitcast.7) | data formatting | bytes 1769472 | tf_op jit(solution)/shard_map/reshape | solution.py:413

commit v5 on v4

--- a/solution.py
+++ b/solution.py
@@ -24,7 +24,7 @@
 
 def parts_of(packed):
     units = packed // 16
-    b = round(units * 2 / 9)
+    b = round(units * 0.15)
     a = units - b
     cuts = [0, (a + 1) // 2, a, a + (b + 1) // 2, units]
     cuts = [16 * c for c in cuts]
@@ -54,7 +54,7 @@
     tokens_ref, vectors_ref, keep_ref, rows_ref, w_ref,
     out_ref,
     own, wbuf, hid, ends_upper, ends_lower, spread, returns, full, state, pieces, total,
-    send_sems, in_sems, swap_send, swap_recv, piece_sems, total_sems, local_sem,
+    send_sems, in_sems, swap_send, swap_recv, sum_sems, piece_sems, total_sems, local_sem,
 ):
     n_img, n_seq, grid_rows, grid_cols, depth, width, inner = dims
     main_tiles = depth // LANES
@@ -75,7 +75,13 @@
     left = gray(lax.rem(ring + 3, 4))
     far = gray(lax.rem(ring + 2, 4))
     twin = seq + 1 - 2 * core
-    zs = [z, z + 1 - 2 * lax.rem(z, 2), 2 - z // 2, 3 - 3 * (z // 2)]
+    zs = [
+        jnp.where(z == 0, 1, z),
+        jnp.where(z == 0, 2, jnp.where(z == 2, 3, 2)),
+        jnp.where(z < 2, 3, 1),
+        jnp.zeros_like(z),
+    ]
+    arrivals = [jnp.where(z == 0, zs[k], zs[k + 1]) for k in range(n_z - 1)]
     mine = [2 * q + core for q in zs]
     twins = [2 * q + 1 - core for q in zs]
 
@@ -135,9 +141,8 @@
         for span in spans:
             arrive(i, q, span, in_sems.at[i, q, slot[span]])
 
-    def give(src, i, q, to, *spans):
-        for span in spans:
-            send(src, i, q, span, in_sems.at[i, q, slot[span]], to, seq)
+    def give(src, i, q, to, span, when=None):
+        send(src, i, q, span, in_sems.at[i, q, slot[span]], to, seq, when)
 
     def start_line(src, i, spans):
         for span in spans:
@@ -157,9 +162,9 @@
 
     keep_own = pltpu.make_async_copy(own, wbuf.at[img, z], local_sem)
     keep_own.start()
-    for span in (A0, A1):
-        give(own, img, z, right, span)
-        give(own, img, z, left, span)
+    for span, when in ((A0, None), (A1, z > 0)):
+        give(own, img, z, right, span, when)
+        give(own, img, z, left, span, when)
         start_line(own, img, [span])
     for span in (B0, B1):
         give(own, img, z, right, span)
@@ -245,9 +250,13 @@
             get(i, q, B)
             relay(block_of(i, q), i, q, [B])
 
+    def twin_done(k):
+        rows = full.at[pl.ds(pl.multiple_of(twins[k] * width, width), width)]
+        swap(2 + k, rows, rows).wait_recv()
+
     for k in range(n_z):
         if k + 1 < n_z:
-            q = zs[k + 1]
+            q = arrivals[k]
             src = block_of(img, q)
             for span in (A0, A1):
                 get(img, q, span)
@@ -256,38 +265,35 @@
                 relay(src, img, q, [span])
             get(img, q, B)
             relay(src, img, q, [B])
+        if k + 2 == n_z:
+            give(own, img, z, right, A1, z == 0)
+            give(own, img, z, left, A1, z == 0)
         q = zs[k]
-        from_left, from_right, from_far = block_of(left, q), block_of(right, q), block_of(far, q)
+        from_left, from_right = block_of(left, q), block_of(right, q)
         get(left, q, A0)
         give(from_left, left, q, right, A0)
         get(right, q, A0, A1)
         give(from_right, right, q, left, A1)
         get(left, q, A1)
         if k == 0:
-            get(left, q, B0)
-            give(from_left, left, q, right, B0)
-            get(right, q, B0, B1)
-            give(from_right, right, q, left, B1)
-            start_line(from_right, right, [B])
-            get(left, q, B1)
-            start_line(from_left, left, [B])
-        elif k == 1:
-            side_rows(q)
-        elif k == 2:
-            side_rows(q)
-            side_rows(zs[3])
-        get(far, q, A0, A1)
-        if k == 0:
-            get(far, q, B0, B1)
-            start_line(from_far, far, [B])
-        else:
-            finish(k - 1)
-    finish(n_z - 1)
-
-    for k in range(n_z):
-        rows = full.at[pl.ds(pl.multiple_of(twins[k] * width, width), width)]
-        swap(2 + k, rows, rows).wait_recv()
-
+            get(left, z, B0)
+            give(block_of(left, z), left, z, right, B0)
+            get(right, z, B0, B1)
+            give(block_of(right, z), right, z, left, B1)
+            get(left, z, B1)
+            get(far, q, A0, A1)
+            continue
+        if k == 1:
+            get(far, z, B0, B1)
+            for i in (left, right, far):
+                start_line(block_of(i, z), i, [B])
+        side_rows(arrivals[k - 1])
+        finish(k - 1)
+        if k + 1 < n_z:
+            get(far, q, A0, A1)
+
+    for k in range(n_z - 1):
+        twin_done(k)
     groups = inner // LANES
     head_of_row = lax.broadcasted_iota(jnp.int32, (LANES, LANES), 0) // HDIM
     head_of_col = lax.broadcasted_iota(jnp.int32, (LANES, LANES), 1) // HDIM
@@ -316,11 +322,13 @@
         to = lax.rem(seq + d, n_seq)
         copy = pltpu.make_async_remote_copy(
             src_ref=piece_of(state, to), dst_ref=pieces.at[d - 1],
-            send_sem=send_sems.at[len(sends) + d - 1], recv_sem=piece_sems.at[d - 1],
+            send_sem=sum_sems.at[0, d - 1], recv_sem=piece_sems.at[d - 1],
             device_id={"img": img, "seq": to}, device_id_type=pl.DeviceIdType.MESH,
         )
         copy.start()
         scattered.append(copy)
+    get(far, zs[n_z - 1], A0, A1)
+    finish(n_z - 1)
     summed = state[pl.ds(pl.multiple_of(seq * piece, piece), piece), :]
     for d in range(1, n_seq):
         scattered[d - 1].wait_recv()
@@ -329,11 +337,12 @@
     for d in range(1, n_seq):
         copy = pltpu.make_async_remote_copy(
             src_ref=piece_of(total, seq), dst_ref=piece_of(total, seq),
-            send_sem=send_sems.at[len(sends) + n_seq - 1 + d - 1], recv_sem=total_sems.at[d - 1],
+            send_sem=sum_sems.at[1, d - 1], recv_sem=total_sems.at[d - 1],
             device_id={"img": img, "seq": lax.rem(seq + d, n_seq)}, device_id_type=pl.DeviceIdType.MESH,
         )
         copy.start()
         gathered.append(copy)
+    twin_done(n_z - 1)
     for d in range(1, n_seq):
         block = piece_of(total, lax.rem(seq + n_seq - d, n_seq))
         pltpu.make_async_remote_copy(
@@ -395,6 +404,7 @@
             dma((n_img, n_z, 4)),
             dma((2 + n_z,)),
             dma((2 + n_z,)),
+            dma((2, n_seq - 1)),
             dma((n_seq - 1,)),
             dma((n_seq - 1,)),
             dma(()),

time: 111 us -> 103 us (0.928)
  Pallas kernels: 104 us -> 96.8 us
    pallas_call x1, Pallas kernels: 104 us -> 96.8 us  [fast_body(): pl.pallas_call(functools.partial(kernel, dims), out_shape=jax.ShapeDtypeS...]
where the time goes in v5:
time: 103 us
  Pallas kernels  96.8 us (94%)
  local copies, waits for them, and re-layouts  3.62 us (4%)
  other arithmetic  1.34 us (1%)
  between operations  1.31 us (1%)
    pallas_call x1, Pallas kernels, fast_body(): pl.pallas_call(functools.partial(kernel, dims), out_shape=jax.ShapeDtypeS...  96.8 us
    reshape x1, local copies, waits for them, and re-layouts, fast_body(): return out.transpose(0, 2, 1).reshape(1, grid_rows, grid_cols, inner)  2.22 us

profile of v5, /device:TPU:0, one launch (start us, length us, event | category | flops | bytes accessed | tf_op | source)
XLA Modules:
  0.0 103.1 jit_solution(10927721450349175705)
XLA Ops:
  1.3 0.7 stack.9
  2.0 0.7 stack.10
  2.7 1.3 %pad_maximum_fusion.vectors_ref = bf16[3,2240]{1,0:T(4,128)(2,1)} fusion(bf16[1,2240]{1,0:T(2,128)(2,1)S(1)} %stack.10, bf16[1,2240]{1,0:T(2,128)(2,1)} %param.9, bf16[1,2240]{1,0:T(2,128)(2,1)S(1)} %stack.9), kind=kLoop, calls=%fused_computation | loop fusion | flops 40320 | bytes 26880 | tf_op jit(solution)/shard_map/stack | solution.py:421
  4.0 96.8 %shard_map.73 = bf16[3,1152,128]{2,1,0:T(8,128)(2,1)} custom-call(bf16[3,2240,128]{2,1,0:T(8,128)(2,1)} %bitcast.8, bf16[3,2240]{1,0:T(4,128)(2,1)} %pad_maximum_fusion.vectors_ref, s32[1]{0:T(128)S(6)} %copy.9.keep_ref, s32[1]{0:T(128)S(6)} %copy.10.rows_ref, bf16[432,560]{1,0:T(8,128)(2,1)} %bitcast.9), custom_call_target="tpu_custom_call" | custom-call | flops 5945425920 | bytes 3440640 | tf_op jit(solution)/shard_map/pallas_call | solution.py:386
  100.8 2.2 %copy.8 = bf16[1,3,128,1152]{3,2,1,0:T(8,128)(2,1)} copy(bf16[1,3,128,1152]{2,3,1,0:T(8,128)(2,1)} %bitcast.7) | data formatting | bytes 1769472 | tf_op jit(solution)/shard_map/reshape | solution.py:423

commit v6 on v5

--- a/solution.py
+++ b/solution.py
@@ -23,16 +23,8 @@
 
 
 def parts_of(packed):
-    units = packed // 16
-    b = round(units * 0.15)
-    a = units - b
-    cuts = [0, (a + 1) // 2, a, a + (b + 1) // 2, units]
-    cuts = [16 * c for c in cuts]
-
-    def span(i, j):
-        return (cuts[i], cuts[j] - cuts[i])
-
-    return span(0, 2), span(0, 1), span(1, 2), span(2, 4), span(2, 3), span(3, 4)
+    half = -(-packed // 32) * 16
+    return (0, half), (half, packed - half)
 
 
 def product(a, b, dims):
@@ -62,7 +54,7 @@
     tail = depth - main
     top = half_rows(width)
     packed = own.shape[0]
-    A, A0, A1, B, B0, B1 = parts_of(packed)
+    A0, A1 = parts_of(packed)
     n_z = n_seq // 2
     token_count = grid_rows * grid_cols
 
@@ -135,7 +127,7 @@
             device_id={"img": img, "seq": twin}, device_id_type=pl.DeviceIdType.MESH,
         ).wait_recv()
 
-    slot = {A0: 0, A1: 1, B0: 2, B1: 3, B: 2}
+    slot = {A0: 0, A1: 1}
 
     def get(i, q, *spans):
         for span in spans:
@@ -166,10 +158,6 @@
         give(own, img, z, right, span, when)
         give(own, img, z, left, span, when)
         start_line(own, img, [span])
-    for span in (B0, B1):
-        give(own, img, z, right, span)
-        give(own, img, z, left, span)
-    start_line(own, img, [B])
 
     flag = jnp.full((1, depth * n_img), keep_ref[0])
     condition = jnp.where(flag > 0, vectors_ref[1:2, :].astype(jnp.float32), vectors_ref[2:3, :].astype(jnp.float32))
@@ -245,29 +233,20 @@
                 ]
         project(k)
 
-    def side_rows(q):
-        for i in (left, right, far):
-            get(i, q, B)
-            relay(block_of(i, q), i, q, [B])
-
     def twin_done(k):
         rows = full.at[pl.ds(pl.multiple_of(twins[k] * width, width), width)]
         swap(2 + k, rows, rows).wait_recv()
 
-    for k in range(n_z):
-        if k + 1 < n_z:
-            q = arrivals[k]
-            src = block_of(img, q)
-            for span in (A0, A1):
-                get(img, q, span)
-                give(src, img, q, right, span)
-                give(src, img, q, left, span)
-                relay(src, img, q, [span])
-            get(img, q, B)
-            relay(src, img, q, [B])
-        if k + 2 == n_z:
-            give(own, img, z, right, A1, z == 0)
-            give(own, img, z, left, A1, z == 0)
+    def pass_on(k):
+        q = arrivals[k]
+        src = block_of(img, q)
+        for span in (A0, A1):
+            get(img, q, span)
+            give(src, img, q, right, span)
+            give(src, img, q, left, span)
+            relay(src, img, q, [span])
+
+    def go_round(k):
         q = zs[k]
         from_left, from_right = block_of(left, q), block_of(right, q)
         get(left, q, A0)
@@ -275,22 +254,19 @@
         get(right, q, A0, A1)
         give(from_right, right, q, left, A1)
         get(left, q, A1)
-        if k == 0:
-            get(left, z, B0)
-            give(block_of(left, z), left, z, right, B0)
-            get(right, z, B0, B1)
-            give(block_of(right, z), right, z, left, B1)
-            get(left, z, B1)
-            get(far, q, A0, A1)
-            continue
-        if k == 1:
-            get(far, z, B0, B1)
-            for i in (left, right, far):
-                start_line(block_of(i, z), i, [B])
-        side_rows(arrivals[k - 1])
-        finish(k - 1)
-        if k + 1 < n_z:
-            get(far, q, A0, A1)
+
+    pass_on(0)
+    for k in range(n_z - 1):
+        go_round(k)
+        if k + 2 < n_z:
+            pass_on(k + 1)
+        if k + 3 == n_z:
+            give(own, img, z, right, A1, z == 0)
+            give(own, img, z, left, A1, z == 0)
+        if k > 0:
+            finish(k - 1)
+        get(far, zs[k], A0, A1)
+    finish(n_z - 2)
 
     for k in range(n_z - 1):
         twin_done(k)
@@ -327,6 +303,7 @@
         )
         copy.start()
         scattered.append(copy)
+    go_round(n_z - 1)
     get(far, zs[n_z - 1], A0, A1)
     finish(n_z - 1)
     summed = state[pl.ds(pl.multiple_of(seq * piece, piece), piece), :]
@@ -401,7 +378,7 @@
             pltpu.VMEM((n_seq - 1, piece, LANES), jnp.float32),
             pltpu.VMEM((piece * n_seq, LANES), jnp.float32),
             dma((192,)),
-            dma((n_img, n_z, 4)),
+            dma((n_img, n_z, 2)),
             dma((2 + n_z,)),
             dma((2 + n_z,)),
             dma((2, n_seq - 1)),

time: 103 us -> 99.6 us (0.967)
  Pallas kernels: 96.8 us -> 93 us
    pallas_call x1, Pallas kernels: 96.8 us -> 93 us  [fast_body(): pl.pallas_call(functools.partial(kernel, dims), out_shape=jax.ShapeDtypeS...]
where the time goes in v6:
time: 99.6 us; the launch traced here: 99.3 us
  Pallas kernels  93 us (93%)
  local copies, waits for them, and re-layouts  3.62 us (4%)
  other arithmetic  1.34 us (1%)
  between operations  1.31 us (1%)
    pallas_call x1, Pallas kernels, fast_body(): pl.pallas_call(functools.partial(kernel, dims), out_shape=jax.ShapeDtypeS...  93 us
    reshape x1, local copies, waits for them, and re-layouts, fast_body(): return out.transpose(0, 2, 1).reshape(1, grid_rows, grid_cols, inner)  2.22 us

profile of v6, /device:TPU:0, one launch (start us, length us, event | category | flops | bytes accessed | tf_op | source)
XLA Modules:
  0.0 99.3 jit_solution(3075087107506118643)
XLA Ops:
  1.3 0.7 stack.9
  2.0 0.7 stack.10
  2.7 1.3 %pad_maximum_fusion.vectors_ref = bf16[3,2240]{1,0:T(4,128)(2,1)} fusion(bf16[1,2240]{1,0:T(2,128)(2,1)S(1)} %stack.10, bf16[1,2240]{1,0:T(2,128)(2,1)} %param.9, bf16[1,2240]{1,0:T(2,128)(2,1)S(1)} %stack.9), kind=kLoop, calls=%fused_computation | loop fusion | flops 40320 | bytes 26880 | tf_op jit(solution)/shard_map/stack | solution.py:398
  4.0 93.0 %shard_map.73 = bf16[3,1152,128]{2,1,0:T(8,128)(2,1)} custom-call(bf16[3,2240,128]{2,1,0:T(8,128)(2,1)} %bitcast.8, bf16[3,2240]{1,0:T(4,128)(2,1)} %pad_maximum_fusion.vectors_ref, s32[1]{0:T(128)S(6)} %copy.9.keep_ref, s32[1]{0:T(128)S(6)} %copy.10.rows_ref, bf16[432,560]{1,0:T(8,128)(2,1)} %bitcast.9), custom_call_target="tpu_custom_call" | custom-call | flops 5945425920 | bytes 3440640 | tf_op jit(solution)/shard_map/pallas_call | solution.py:363
  97.0 2.2 %copy.8 = bf16[1,3,128,1152]{3,2,1,0:T(8,128)(2,1)} copy(bf16[1,3,128,1152]{2,3,1,0:T(8,128)(2,1)} %bitcast.7) | data formatting | bytes 1769472 | tf_op jit(solution)/shard_map/reshape | solution.py:400

commit v7 on v6

--- a/solution.py
+++ b/solution.py
@@ -23,8 +23,16 @@
 
 
 def parts_of(packed):
-    half = -(-packed // 32) * 16
-    return (0, half), (half, packed - half)
+    units = packed // 16
+    b = round(units * 0.15)
+    a = units - b
+    cuts = [0, (a + 1) // 2, a, a + (b + 1) // 2, units]
+    cuts = [16 * c for c in cuts]
+
+    def span(i, j):
+        return (cuts[i], cuts[j] - cuts[i])
+
+    return span(0, 2), span(0, 1), span(1, 2), span(2, 4), span(2, 3), span(3, 4)
 
 
 def product(a, b, dims):
@@ -54,7 +62,7 @@
     tail = depth - main
     top = half_rows(width)
     packed = own.shape[0]
-    A0, A1 = parts_of(packed)
+    A, A0, A1, B, B0, B1 = parts_of(packed)
     n_z = n_seq // 2
     token_count = grid_rows * grid_cols
 
@@ -127,7 +135,7 @@
             device_id={"img": img, "seq": twin}, device_id_type=pl.DeviceIdType.MESH,
         ).wait_recv()
 
-    slot = {A0: 0, A1: 1}
+    slot = {A0: 0, A1: 1, B0: 2, B1: 3, B: 2}
 
     def get(i, q, *spans):
         for span in spans:
@@ -158,6 +166,10 @@
         give(own, img, z, right, span, when)
         give(own, img, z, left, span, when)
         start_line(own, img, [span])
+    for span in (B0, B1):
+        give(own, img, z, right, span)
+        give(own, img, z, left, span)
+    start_line(own, img, [B])
 
     flag = jnp.full((1, depth * n_img), keep_ref[0])
     condition = jnp.where(flag > 0, vectors_ref[1:2, :].astype(jnp.float32), vectors_ref[2:3, :].astype(jnp.float32))
@@ -233,6 +245,11 @@
                 ]
         project(k)
 
+    def side_rows(q):
+        for i in (left, right, far):
+            get(i, q, B)
+            relay(block_of(i, q), i, q, [B])
+
     def twin_done(k):
         rows = full.at[pl.ds(pl.multiple_of(twins[k] * width, width), width)]
         swap(2 + k, rows, rows).wait_recv()
@@ -245,6 +262,8 @@
             give(src, img, q, right, span)
             give(src, img, q, left, span)
             relay(src, img, q, [span])
+        get(img, q, B)
+        relay(src, img, q, [B])
 
     def go_round(k):
         q = zs[k]
@@ -258,14 +277,26 @@
     pass_on(0)
     for k in range(n_z - 1):
         go_round(k)
+        if k == 0:
+            get(left, z, B0)
+            give(block_of(left, z), left, z, right, B0)
+            get(right, z, B0, B1)
+            give(block_of(right, z), right, z, left, B1)
+            get(left, z, B1)
         if k + 2 < n_z:
             pass_on(k + 1)
         if k + 3 == n_z:
             give(own, img, z, right, A1, z == 0)
             give(own, img, z, left, A1, z == 0)
+        if k == 1:
+            get(far, z, B0, B1)
+            for i in (left, right, far):
+                start_line(block_of(i, z), i, [B])
         if k > 0:
+            side_rows(arrivals[k - 1])
             finish(k - 1)
         get(far, zs[k], A0, A1)
+    side_rows(arrivals[n_z - 2])
     finish(n_z - 2)
 
     for k in range(n_z - 1):
@@ -378,7 +409,7 @@
             pltpu.VMEM((n_seq - 1, piece, LANES), jnp.float32),
             pltpu.VMEM((piece * n_seq, LANES), jnp.float32),
             dma((192,)),
-            dma((n_img, n_z, 2)),
+            dma((n_img, n_z, 4)),
             dma((2 + n_z,)),
             dma((2 + n_z,)),
             dma((2, n_seq - 1)),

time: 99.6 us -> 104 us (1.044)
  Pallas kernels: 93 us -> 97 us
    pallas_call x1, Pallas kernels: 93 us -> 97 us  [fast_body(): pl.pallas_call(functools.partial(kernel, dims), out_shape=jax.ShapeDtypeS...]
where the time goes in v7:
time: 104 us; the launch traced here: 103 us
  Pallas kernels  97 us (93%)
  local copies, waits for them, and re-layouts  3.62 us (3%)
  other arithmetic  1.34 us (1%)
  between operations  1.31 us (1%)
    pallas_call x1, Pallas kernels, fast_body(): pl.pallas_call(functools.partial(kernel, dims), out_shape=jax.ShapeDtypeS...  97 us
    reshape x1, local copies, waits for them, and re-layouts, fast_body(): return out.transpose(0, 2, 1).reshape(1, grid_rows, grid_cols, inner)  2.22 us

profile of v7, /device:TPU:0, one launch (start us, length us, event | category | flops | bytes accessed | tf_op | source)
XLA Modules:
  0.0 103.3 jit_solution(8420220572426639402)
XLA Ops:
  1.3 0.7 stack.9
  2.0 0.7 stack.10
  2.7 1.3 %pad_maximum_fusion.vectors_ref = bf16[3,2240]{1,0:T(4,128)(2,1)} fusion(bf16[1,2240]{1,0:T(2,128)(2,1)S(1)} %stack.10, bf16[1,2240]{1,0:T(2,128)(2,1)} %param.9, bf16[1,2240]{1,0:T(2,128)(2,1)S(1)} %stack.9), kind=kLoop, calls=%fused_computation | loop fusion | flops 40320 | bytes 26880 | tf_op jit(solution)/shard_map/stack | solution.py:429
  4.0 97.0 %shard_map.73 = bf16[3,1152,128]{2,1,0:T(8,128)(2,1)} custom-call(bf16[3,2240,128]{2,1,0:T(8,128)(2,1)} %bitcast.8, bf16[3,2240]{1,0:T(4,128)(2,1)} %pad_maximum_fusion.vectors_ref, s32[1]{0:T(128)S(6)} %copy.9.keep_ref, s32[1]{0:T(128)S(6)} %copy.10.rows_ref, bf16[432,560]{1,0:T(8,128)(2,1)} %bitcast.9), custom_call_target="tpu_custom_call" | custom-call | flops 5945425920 | bytes 3440640 | tf_op jit(solution)/shard_map/pallas_call | solution.py:394
  101.1 2.2 %copy.8 = bf16[1,3,128,1152]{3,2,1,0:T(8,128)(2,1)} copy(bf16[1,3,128,1152]{2,3,1,0:T(8,128)(2,1)} %bitcast.7) | data formatting | bytes 1769472 | tf_op jit(solution)/shard_map/reshape | solution.py:431
